TPU v7x, 512 devices: a whole 4x8x8 slice. The times are simulated.
512 devices in a mesh: nodes: 128 (over z, y, core), grp: 4 (over x).
Axes of the slice: x: 4, y: 8, z: 8, core: 2. Of those that a mesh axis runs over, the one named last changes fastest.
Arguments:
- grad_out: bfloat16 [393216, 128], P(('nodes', 'grp')), may hold values from -6 to 6
- agg_saved: bfloat16 [393216, 128], P(('nodes', 'grp')), may hold values from -6 to 6
- hidden_saved: bfloat16 [393216, 256], P(('nodes', 'grp')), may hold values from 0 to 6
- w_one: bfloat16 [128, 256], replicated, may hold values from -0.5 to 0.5
- w_two: bfloat16 [256, 128], replicated, may hold values from -0.375 to 0.375
- local_lists: int32 [393216, 16], P(('nodes', 'grp')), may hold values from 0 to 768
- send_slots: int32 [128, 4, 128, 4, 8], P('nodes', 'grp'), may hold values from 0 to 768, as said below
- receive_slots: int32 [128, 4, 128, 4, 8], P('nodes', 'grp'), may hold values from 0 to 768, as said below
Outputs:
- grad_x: bfloat16 [393216, 128], P(('nodes', 'grp'))
- grad_w1: float32 [128, 256], replicated
- grad_b1: float32 [256], replicated
- grad_w2: float32 [256, 128], replicated
- grad_b2: float32 [128], replicated
- grad_vn: float32 [128], replicated
Inputs may be any that keep to these rules, and one draw needn't show every extreme that they name: For each sender and receiver the filled slots of send_slots and receive_slots are the same ones; some receivers get all 8 slots filled from every sender. `receive_slots`: filled exactly where send_slots is filled for the same pair of devices.
All inputs are finite; a program needn't handle non-finite values.
Results may differ from a plain program's by a relative error of at most 0.007.
Values may be sent and summed in bfloat16 or wider, within the bound.
No kernel may reach another device: no remote copies, remote signals or barrier semaphores. Data moves between devices by JAX's collectives and lax.ppermute only.
A program may use at most 64 MiB of HBM per device.

v0:
```python
import jax
import jax.numpy as jnp
from jax import lax
from jax.sharding import PartitionSpec as P


def per_device(
    grad_out, agg_saved, hidden_saved, w_one, w_two, local_lists, send_slots, receive_slots
):
    row_count = grad_out.shape[0]
    width = grad_out.shape[1]
    contract_last = (((1,), (1,)), ((), ()))
    contract_first = (((0,), (0,)), ((), ()))
    grad_hidden = lax.dot_general(
        grad_out, w_two, contract_last, preferred_element_type=jnp.float32
    )
    grad_z = jnp.where(hidden_saved > 0, grad_hidden, jnp.zeros_like(grad_hidden)).astype(
        jnp.bfloat16
    )
    grad_agg = lax.dot_general(grad_z, w_one, contract_last, preferred_element_type=jnp.float32)
    part_w2 = lax.dot_general(
        hidden_saved, grad_out, contract_first, preferred_element_type=jnp.float32
    )
    part_b2 = jnp.sum(grad_out.astype(jnp.float32), axis=0)
    part_w1 = lax.dot_general(agg_saved, grad_z, contract_first, preferred_element_type=jnp.float32)
    part_b1 = jnp.sum(grad_z.astype(jnp.float32), axis=0)
    agg_wire = grad_agg.astype(jnp.bfloat16)
    padded = jnp.concatenate([agg_wire, jnp.zeros((1, width), jnp.bfloat16)], axis=0)
    sender_rows = send_slots[0, 0]
    target_rows = receive_slots[0, 0]
    device_count = lax.axis_size("nodes") * lax.axis_size("grp")
    scale = 1.0 / device_count
    messages = padded[sender_rows]
    arrived = lax.all_to_all(
        lax.all_to_all(messages, "nodes", split_axis=0, concat_axis=0, tiled=True),
        "grp",
        split_axis=1,
        concat_axis=1,
        tiled=True,
    )
    total = grad_agg
    for column in range(local_lists.shape[1]):
        total = total + padded[local_lists[:, column]].astype(jnp.float32)
    remote = (
        jnp.zeros((row_count + 1, width), jnp.float32)
        .at[target_rows.reshape(-1)]
        .add(arrived.reshape(-1, width).astype(jnp.float32))
    )
    total = total + remote[:row_count]
    grad_x = total.astype(jnp.bfloat16)
    sum_w1, sum_b1, sum_w2, sum_b2 = lax.psum(
        (part_w1, part_b1, part_w2, part_b2), ("nodes", "grp")
    )
    sum_node = lax.psum(jnp.sum(total, axis=0), ("nodes", "grp"))
    return (
        grad_x,
        sum_w1 * scale,
        sum_b1 * scale,
        sum_w2 * scale,
        sum_b2 * scale,
        sum_node * scale,
    )


def solution(mesh):
    placed = (
        P(("nodes", "grp"), None),
        P(("nodes", "grp"), None),
        P(("nodes", "grp"), None),
        P(),
        P(),
        P(("nodes", "grp"), None),
        P("nodes", "grp", None, None, None),
        P("nodes", "grp", None, None, None),
    )
    return jax.shard_map(
        per_device,
        mesh=mesh,
        in_specs=placed,
        out_specs=(P(("nodes", "grp"), None), P(), P(), P(), P(), P()),
        check_vma=False,
    )
```

profile of v0, /device:TPU:1, one launch (start us, length us, event | category | flops | bytes accessed | tf_op | source)
XLA Modules:
  0.0 457.1 jit_solution(14423630005700525120)
XLA Ops:
  7.2 0.8 compare_select_fusion.1
  8.3 1.5 convert_reduce_fusion
  9.8 1.8 fusion.20
  11.7 14.9 %gather_fusion.16 = bf16[4096,128]{1,0:T(8,128)(2,1)} fusion(bf16[769,128]{1,0:T(8,128)(2,1)S(1)} %concatenate.3, s32[4096]{0:T(1024)S(1)} %broadcast_clamp_fusion), kind=kCustom, calls=%fused_computation.16 | custom fusion | bytes 2113536 | tf_op jit(solution)/shard_map/gather | solution.py:33
  26.6 18.6 %all-to-all-start = ((bf16[128,4,8,128]{3,2,1,0:T(8,128)(2,1)}), bf16[128,4,8,128]{3,2,1,0:T(8,128)(2,1)S(1)}, u32[]{:S(2)}, u32[]{:S(2)}) async-start(bf16[128,4,8,128]{3,2,1,0:T(8,128)(2,1)} %bitcast.2), calls=%async_computation | async-start | bytes 2097152 | tf_op jit(solution)/shard_map/all_to_all | solution.py:35
  45.2 1.0 fusion.21
  46.2 1.0 convolution_bitcast_fusion
  48.5 27.6 %all-to-all-done = bf16[128,4,8,128]{3,2,1,0:T(8,128)(2,1)S(1)} async-done(((bf16[128,4,8,128]{3,2,1,0:T(8,128)(2,1)}), bf16[128,4,8,128]{3,2,1,0:T(8,128)(2,1)S(1)}, u32[]{:S(2)}, u32[]{:S(2)}) %all-to-all-start) | async-done | bytes 1048608 | tf_op jit(solution)/shard_map/all_to_all | solution.py:35
  76.1 1.2 copy.25
  77.3 4.0 all-to-all-start.1
  81.3 2.5 gather_fusion.15
  83.8 2.5 gather_fusion.14
  86.3 2.5 gather_fusion.13
  88.9 2.5 gather_fusion.12
  91.4 2.5 gather_fusion.11
  93.9 2.5 gather_fusion.10
  96.4 2.5 gather_fusion.9
  98.9 2.5 gather_fusion.8
  101.4 2.5 gather_fusion.7
  103.9 2.5 gather_fusion.6
  106.4 2.5 gather_fusion.5
  108.9 2.5 gather_fusion.4
  111.4 2.5 gather_fusion.3
  113.9 2.5 gather_fusion.2
  116.4 2.5 gather_fusion.1
  118.9 2.5 gather_fusion
  121.6 200.5 %all-reduce.5.cloned.1.call-done = (f32[128,256]{0,1:T(8,128)}, f32[256,128]{1,0:T(8,128)}) async-done(((f32[128,256]{0,1:T(8,128)}, f32[256,128]{1,0:T(8,128)}), (f32[128,256]{0,1:T(8,128)}, f32[256,128]{1,0:T(8,128)})) %all-reduce.5.cloned.1.call-update) | async-done | bytes 262160 | tf_op jit(solution)/shard_map/psum | solution.py:51
  322.1 0.9 broadcast_multiply_fusion.1
  323.8 1.6 broadcast_multiply_fusion
  325.6 22.6 %scatter_custom_fusion = f32[769,128]{1,0:T(8,128)S(1)} fusion(s32[4096]{0:T(1024)} %bitcast.18, f32[4096,128]{1,0:T(8,128)S(1)} %bitcast.17, f32[]{:T(128)} %constant.6.clone.1), kind=kCustom, calls=%fused_computation.24 | custom fusion | flops 524288 | bytes 394240 | tf_op jit(solution)/shard_map/scatter-add | solution.py:47
  348.3 3.2 fusion.19
  351.4 97.2 %all-reduce.1 = (f32[256]{0:T(256)S(1)}, f32[128]{0:T(128)S(1)}, f32[128]{0:T(128)S(1)}) all-reduce(f32[256]{0:T(256)S(1)} %get-tuple-element.55, f32[128]{0:T(128)S(1)} %convert_reduce_fusion.1, f32[128]{0:T(128)S(1)} %get-tuple-element.51), channel_id=1, replica_groups=mesh['nodes'=128,'grp'=4] {'nodes','grp'}, use_global_device_ids=true, to_apply=%region_3.4 | all-reduce | flops 512 | bytes 4096 | tf_op jit(solution)/shard_map/psum | solution.py:51
  (37 shorter events, 4.5 us)
Async XLA Ops:
  7.2 39.0 %copy-start = (bf16[768,128]{1,0:T(8,128)(2,1)S(1)}, bf16[768,128]{1,0:T(8,128)(2,1)}, u32[]{:S(2)}) copy-start(bf16[768,128]{1,0:T(8,128)(2,1)} %param.9) | copy-start | bytes 589828
  26.6 18.6 %copy-start.2 = (bf16[768,128]{1,0:T(8,128)(2,1)S(1)}, bf16[768,128]{1,0:T(8,128)(2,1)}, u32[]{:S(2)}) copy-start(bf16[768,128]{1,0:T(8,128)(2,1)} %param.8) | copy-start | bytes 589828
  26.6 18.7 %copy-start.3 = (bf16[768,256]{1,0:T(8,128)(2,1)S(1)}, bf16[768,256]{1,0:T(8,128)(2,1)}, u32[]{:S(2)}) copy-start(bf16[768,256]{1,0:T(8,128)(2,1)} %param.10) | copy-start | bytes 1179652
  26.6 20.6 %copy-start.5 = (s32[1,1,128,4,8]{2,4,3,1,0:T(8,128)S(1)}, s32[1,1,128,4,8]{2,4,3,1,0:T(8,128)}, u32[]{:S(2)}) copy-start(s32[1,1,128,4,8]{2,4,3,1,0:T(8,128)} %param.15) | copy-start | bytes 49156
  26.6 21.0 %copy-start.4 = (s32[768,16]{0,1:T(8,128)S(1)}, s32[768,16]{0,1:T(8,128)}, u32[]{:S(2)}) copy-start(s32[768,16]{0,1:T(8,128)} %param.13) | copy-start | bytes 147460
  26.6 49.5 %all-to-all-start = ((bf16[128,4,8,128]{3,2,1,0:T(8,128)(2,1)}), bf16[128,4,8,128]{3,2,1,0:T(8,128)(2,1)S(1)}, u32[]{:S(2)}, u32[]{:S(2)}) async-start(bf16[128,4,8,128]{3,2,1,0:T(8,128)(2,1)} %bitcast.2), calls=%async_computation | async-start | bytes 2097152 | tf_op jit(solution)/shard_map/all_to_all | solution.py:35
  45.2 276.9 %all-reduce.5.cloned.1.call-start = ((), (), s32[]{:S(2)}) async-start(), calls=%async_computation.2 | async-start | bytes 524288 | tf_op jit(solution)/shard_map/psum | solution.py:51
  77.3 248.1 %all-to-all-start.1 = ((bf16[128,4,8,128]{3,2,0,1:T(8,128)(2,1)}), bf16[128,4,8,128]{3,2,0,1:T(8,128)(2,1)S(1)}, u32[]{:S(2)}, u32[]{:S(2)}) async-start(bf16[128,4,8,128]{3,2,0,1:T(8,128)(2,1)} %copy.25), calls=%async_computation.1 | async-start | bytes 2097152 | tf_op jit(solution)/shard_map/all_to_all | solution.py:34
  323.0 25.3 %copy-start.1 = (bf16[768,128]{1,0:T(8,128)(2,1)S(1)}, bf16[768,128]{1,0:T(8,128)(2,1)}, u32[]{:S(2)}) copy-start(bf16[768,128]{1,0:T(8,128)(2,1)} %gather_fusion.15) | copy-start | bytes 589828
Sparse Core Ops, SparseCore 0:
  51.8 270.2 all-reduce.4
where the time goes:
time: 458 us; the launch traced here: 457 us
  waiting for transfers between devices  228 us (50%)
  blocking collectives  97.2 us (21%)
  local copies, waits for them, and re-layouts  58.1 us (13%)
  other arithmetic  31.6 us (7%)
  starting transfers between devices  22.6 us (5%)
  between operations  14.2 us (3%)
  matrix products  5.22 us (1%)
    psum x1, waiting for transfers between devices, per_device(): lax.psum((part_w1, part_b1, part_w2, part_b2), ('nodes', 'grp'))  201 us
    psum x1, blocking collectives, per_device(): lax.psum((part_w1, part_b1, part_w2, part_b2), ('nodes', 'grp'))  97.2 us
    gather x16, local copies, waits for them, and re-layouts, per_device(): total = total + padded[local_lists[:, column]].astype(jnp.float32)  40.1 us
    all_to_all x1, waiting for transfers between devices, per_device(): lax.all_to_all(messages, 'nodes', split_axis=0, concat_axis=0, tiled=True)  27.6 us
    scatter-add x1, other arithmetic, per_device(): remote = jnp.zeros((row_count + 1, width), jnp.float32).at[target_rows.re...  22.6 us
    all_to_all x1, starting transfers between devices, per_device(): lax.all_to_all(messages, 'nodes', split_axis=0, concat_axis=0, tiled=True)  18.6 us
    gather x1, local copies, waits for them, and re-layouts, per_device(): messages = padded[sender_rows]  14.9 us
  transfers between devices with their start and end apart: 3, of which 2 were waited for; matrix products, arithmetic and copies ran while one was open for 10% of the time, Pallas kernels for 0%

commit v1 on v0

v1 whole, which is shorter than its diff:
```python
import functools

import jax
import jax.numpy as jnp
from jax import lax
from jax.experimental import pallas as pl
from jax.experimental.pallas import tpu as pltpu
from jax.sharding import PartitionSpec as P

BF16 = jnp.bfloat16
F32 = jnp.float32
PLAIN = (((1,), (0,)), ((), ()))
LAST = (((1,), (1,)), ((), ()))
FIRST = (((0,), (0,)), ((), ()))
LANES = 128
EXTRA = 2
AXES = ("nodes", "grp")


def dot(a, b, dims=PLAIN):
    return lax.dot_general(a, b, dims, preferred_element_type=F32)


def iota(shape, dim):
    return lax.broadcasted_iota(jnp.int32, shape, dim)


def code(index):
    return ((LANES + (index & (LANES - 1))) << (index >> 7)).astype(F32)


def match(a, b):
    return jnp.where(a == b, 1.0, 0.0).astype(BF16)


def low_part(value):
    return value - value.astype(BF16).astype(F32)


def columns(row):
    return jnp.broadcast_to(row, (LANES, LANES)).T


def remainders(wide, thin):
    lane = iota(wide.shape, 1)
    low = jnp.where(lane == LANES - 2, thin, low_part(wide))
    return jnp.where(lane == LANES - 1, low_part(thin), low).astype(BF16)


def first_kernel(
    send_ref, lists_ref, out_ref, hid_ref, saved_ref, w1_ref, w2_ref,
    piece_ref, total_ref,
    wire_ref, counts_ref, high_ref, low_ref, wide_ref, sent_ref, place_ref, chosen_ref, mail_ref, node_ref,
):
    groups, slots, nodes = send_ref.shape
    rows = out_ref.shape[0]
    piece = slots + EXTRA
    out = out_ref[...]
    hidden = hid_ref[...]
    grad_hidden = dot(out, w2_ref[...], LAST)
    grad_z = jnp.where(hidden > 0, grad_hidden, 0.0).astype(BF16)
    grad_agg = dot(grad_z, w1_ref[...], LAST)
    wire_ref[...] = grad_agg.astype(BF16)

    row_code = code(iota((rows, LANES), 0)).astype(BF16)
    for tile in range(rows // LANES):
        lists = code(lists_ref[:, tile * LANES : (tile + 1) * LANES]).astype(BF16)
        counts = match(lists[0:1], row_code)
        for k in range(1, lists_ref.shape[0]):
            counts += match(lists[k : k + 1], row_code)
        counts_ref[:, tile * LANES : (tile + 1) * LANES] = counts
    local = dot(wire_ref[...].T, counts_ref[...])
    total = grad_agg + local.T
    total_ref[...] = total
    node_ref[...] = jnp.sum(total, axis=0, keepdims=True)

    part_w1 = dot(saved_ref[...], grad_z, FIRST)
    part_w2 = dot(out, hidden, FIRST)
    sum_z = jnp.sum(grad_z.astype(F32), axis=0, keepdims=True)
    sum_out = jnp.sum(out.astype(F32), axis=0, keepdims=True)
    quarters = [
        (part_w1[:, :LANES], sum_z[:, :LANES]),
        (part_w1[:, LANES:], sum_z[:, LANES:]),
        (part_w2[:, :LANES], sum_out),
    ]
    for q, (wide, thin) in enumerate(quarters):
        high_ref[q * LANES : (q + 1) * LANES, :] = wide.astype(BF16)
        low_ref[q * LANES : (q + 1) * LANES, :] = remainders(wide, columns(thin))
    wide_ref[...] = part_w2[:, LANES:]
    high_ref[3 * LANES :, :] = part_w2[:, LANES:].astype(BF16)

    parts = []
    for g in range(groups):
        parts += [code(send_ref[g]), jnp.zeros((EXTRA, nodes), F32)]
    sent = jnp.concatenate(parts, axis=0)
    sent_ref[...] = jnp.concatenate([sent, pltpu.roll(sent, nodes - 1, 1)], axis=0)
    lane = iota(place_ref.shape, 1)
    place_ref[...] = match(
        iota(place_ref.shape, 0), piece * (lane & (LANES - 1)) + slots + (lane >> 7)
    )
    lane_code = code(iota((16, rows), 1)).astype(BF16)
    block = LANES * piece
    width = LANES // groups
    steps = nodes // width

    @pl.loop(0, steps)
    def _(step):
        sent = pltpu.roll(sent_ref[...], nodes - step * width, 1).astype(BF16)
        for n in range(0, width, 2):
            for r in range(0, 2 * groups * piece, 16):
                column = jnp.broadcast_to(sent[r : r + 16, n : n + 1], (16, rows))
                chosen_ref[n * groups * piece + r : n * groups * piece + r + 16, :] = match(column, lane_code)
        mail = dot(chosen_ref[...], wire_ref[...])
        mail_ref[...] = mail
        node_ref[...] += jnp.sum(mail, axis=0, keepdims=True)

        @pl.when(step == steps - 1)
        def _():
            low_ref[3 * LANES :, :] = remainders(wide_ref[...], columns(node_ref[...]))

        own = pl.ds(pl.multiple_of(step * LANES, LANES), LANES)
        sums = jnp.concatenate([high_ref[own, :], low_ref[own, :]], axis=0)
        piece_ref[pl.ds(pl.multiple_of(step * block, block), block), :] = (
            mail_ref[...] + dot(place_ref[...], sums)
        ).astype(BF16)


def chunk_kernel(piece, scale, arrived_ref, share_ref):
    span = piece * LANES
    lane = iota((16, span), 1)
    place = lane - piece * ((lane * ((1 << 16) // piece + 1)) >> 16)
    pick = match(place, piece - EXTRA + iota((16, span), 0))
    sums = jnp.zeros((16, LANES), F32)
    for start in range(0, arrived_ref.shape[0], span):
        sums += dot(pick, arrived_ref[start : start + span, :])
    high, low = sums[0:1], sums[1:2]
    lane = iota(high.shape, 1)
    last = jnp.sum(jnp.where(lane >= LANES - 2, low, 0.0), axis=1, keepdims=True)
    wide = scale * (high + jnp.where(lane >= LANES - 2, 0.0, low))
    thin = jnp.broadcast_to(scale * last, wide.shape)
    pair = jnp.concatenate([wide.astype(BF16), remainders(wide, thin)], axis=0)
    share_ref[...] = jnp.concatenate([pair] * (share_ref.shape[0] // EXTRA), axis=0)


def remote_kernel(recv_ref, arrived_ref, total_ref, x_ref):
    rows = total_ref.shape[0]
    row_code = code(iota((rows, LANES), 0)).astype(BF16)
    targets = code(recv_ref[...]).astype(BF16)
    total = total_ref[...]
    for r in range(0, recv_ref.shape[0], 2):
        chosen = jnp.concatenate([match(targets[q : q + 1], row_code) for q in (r, r + 1)], axis=1)
        total += dot(chosen, arrived_ref[r * LANES : (r + 2) * LANES, :])
    x_ref[...] = total.astype(BF16)


def last_kernel(share_ref, w1_ref, b1_ref, w2_ref, b2_ref, node_ref, rows_ref):
    rows_ref[...] = share_ref[...].astype(F32)
    half = rows_ref.shape[0] // 2
    high = rows_ref[pl.ds(0, half, 2), :]
    low = rows_ref[pl.ds(1, half, 2), :]
    lane = iota(high.shape, 1)
    wide = high + jnp.where(lane >= LANES - 2, 0.0, low)
    w1_ref[:, :LANES] = wide[:LANES]
    w1_ref[:, LANES:] = wide[LANES : 2 * LANES]
    w2_ref[:LANES, :] = wide[2 * LANES : 3 * LANES].T
    w2_ref[LANES:, :] = wide[3 * LANES :].T
    thin = []
    for q in range(4):
        turned = low[q * LANES : (q + 1) * LANES].T
        thin.append(turned[LANES - 2 : LANES - 1] + turned[LANES - 1 :])
    b1_ref[...] = jnp.concatenate(thin[:2], axis=1)
    b2_ref[...] = thin[2]
    node_ref[...] = thin[3]


def call(kernel, outs, scratch=(), **cost):
    return pl.pallas_call(
        kernel,
        out_shape=[jax.ShapeDtypeStruct(shape, dtype) for shape, dtype in outs],
        scratch_shapes=list(scratch),
        compiler_params=pltpu.CompilerParams(vmem_limit_bytes=24 << 20),
        cost_estimate=pl.CostEstimate(transcendentals=0, **cost),
    )


def per_device(
    grad_out, agg_saved, hidden_saved, w_one, w_two, local_lists, send_slots, receive_slots
):
    rows, width = grad_out.shape
    hidden = hidden_saved.shape[1]
    nodes, groups, slots = send_slots.shape[2:]
    devices = nodes * groups
    piece = slots + EXTRA
    send = jnp.transpose(send_slots[0, 0], (1, 2, 0))
    pieces, total = call(
        first_kernel,
        [((devices * piece, width), BF16), ((rows, width), F32)],
        [
            pltpu.VMEM((rows, width), BF16),
            pltpu.VMEM((rows, rows), BF16),
            pltpu.VMEM((devices, LANES), BF16),
            pltpu.VMEM((devices, LANES), BF16),
            pltpu.VMEM((LANES, LANES), F32),
            pltpu.VMEM((2 * groups * piece, nodes), F32),
            pltpu.VMEM((LANES * piece, 2 * LANES), BF16),
            pltpu.VMEM((LANES * piece, rows), BF16),
            pltpu.VMEM((LANES * piece, width), F32),
            pltpu.VMEM((1, width), F32),
        ],
        flops=2 * (devices * piece + rows) * rows * width,
        bytes_accessed=devices * piece * width * 2,
    )(send, local_lists.T, grad_out, hidden_saved, agg_saved, w_one, w_two)

    def exchange(x, height):
        x = x.reshape(devices, height // 2, 2, width)
        return lax.all_to_all(x, AXES, split_axis=0, concat_axis=0, tiled=True).reshape(-1, width)

    arrived = exchange(pieces, piece)
    (share,) = call(
        functools.partial(chunk_kernel, piece, 1.0 / devices),
        [((devices * EXTRA, width), BF16)],
        flops=2 * 16 * devices * piece * width,
        bytes_accessed=devices * piece * width * 2,
    )(arrived)
    shares = exchange(share, EXTRA)
    recv = jnp.pad(receive_slots[0, 0], ((0, 0), (0, 0), (0, EXTRA)), constant_values=rows)
    (grad_x,) = call(
        remote_kernel,
        [((rows, width), BF16)],
        flops=2 * devices * piece * rows * width,
        bytes_accessed=devices * piece * width * 2,
    )(recv.reshape(-1, LANES), arrived, total)
    w1, b1, w2, b2, node = call(
        last_kernel,
        [
            ((width, hidden), F32),
            ((1, hidden), F32),
            ((hidden, width), F32),
            ((1, width), F32),
            ((1, width), F32),
        ],
        [pltpu.VMEM((devices * EXTRA, width), F32)],
        flops=0,
        bytes_accessed=devices * EXTRA * width * 2,
    )(shares)
    return grad_x, w1, b1[0], w2, b2[0], node[0]


def solution(mesh):
    placed = (
        P(AXES, None),
        P(AXES, None),
        P(AXES, None),
        P(),
        P(),
        P(AXES, None),
        P("nodes", "grp", None, None, None),
        P("nodes", "grp", None, None, None),
    )
    return jax.shard_map(
        per_device,
        mesh=mesh,
        in_specs=placed,
        out_specs=(P(AXES, None), P(), P(), P(), P(), P()),
        check_vma=False,
    )
```

time: 458 us -> 112 us (0.24)
  waiting for transfers between devices: 228 us -> 12 us
  local copies, waits for them, and re-layouts: 58.1 us -> 6.51 us
  blocking collectives: 97.2 us -> 59.7 us
  other arithmetic: 31.6 us -> 0 us
  Pallas kernels: 0 us -> 23.3 us
  between operations: 14.2 us -> 0.69 us
  starting transfers between devices: 22.6 us -> 9.66 us
  matrix products: 5.22 us -> 0 us
    psum x1 -> x0, waiting for transfers between devices: 201 us -> none  [per_device(): lax.psum((part_w1, part_b1, part_w2, part_b2), ('nodes', 'grp'))]
    psum x1 -> x0, blocking collectives: 97.2 us -> none  [per_device(): lax.psum((part_w1, part_b1, part_w2, part_b2), ('nodes', 'grp'))]
    all_to_all x0 -> x1, blocking collectives: none -> 59.7 us  [exchange(): lax.all_to_all(x, AXES, split_axis=0, concat_axis=0, tiled=True)]
    gather x17 -> x0, local copies, waits for them, and re-layouts: 55 us -> none  [the longest x16 40.1 us: per_device(): total = total + padded[local_lists[:, column]].astype(jnp.float32)]
    pallas_call x0 -> x4, Pallas kernels: none -> 23.3 us  [the longest x1 17.4 us: per_device(): call(first_kernel, [((devices * piece, width), BF16), ((rows, width), F32...]
    scatter-add x1 -> x0, other arithmetic: 22.6 us -> none  [per_device(): remote = jnp.zeros((row_count + 1, width), jnp.float32).at[target_rows.re...]
    all_to_all x2 -> x1, waiting for transfers between devices: 27.6 us -> 12 us  [exchange(): lax.all_to_all(x, AXES, split_axis=0, concat_axis=0, tiled=True)]
    all_to_all x2 -> x1, starting transfers between devices: 22.6 us -> 9.66 us  [exchange(): lax.all_to_all(x, AXES, split_axis=0, concat_axis=0, tiled=True)]
  transfers between devices with their start and end apart: 3 -> 1, of which waited for: 2 -> 1; matrix products, arithmetic and copies ran while one was open for 10% -> 0% of each run, Pallas kernels for 0% -> 4%
where the time goes in v1:
time: 112 us
  blocking collectives  59.7 us (53%)
  Pallas kernels  23.3 us (21%)
  waiting for transfers between devices  12 us (11%)
  starting transfers between devices  9.66 us (9%)
  local copies, waits for them, and re-layouts  6.51 us (6%)
    all_to_all x1, blocking collectives, exchange(): lax.all_to_all(x, AXES, split_axis=0, concat_axis=0, tiled=True)  59.7 us
    pallas_call x1, Pallas kernels, per_device(): call(first_kernel, [((devices * piece, width), BF16), ((rows, width), F32...  17.4 us
    all_to_all x1, waiting for transfers between devices, exchange(): lax.all_to_all(x, AXES, split_axis=0, concat_axis=0, tiled=True)  12 us
    all_to_all x1, starting transfers between devices, exchange(): lax.all_to_all(x, AXES, split_axis=0, concat_axis=0, tiled=True)  9.66 us
    unnamed x17, local copies, waits for them, and re-layouts  6.18 us
    pallas_call x1, Pallas kernels, per_device(): call(remote_kernel, [((rows, width), BF16)], flops=2 * devices * piece *...  3.97 us
  transfers between devices with their start and end apart: 1, of which 1 were waited for; matrix products, arithmetic and copies ran while one was open for 0% of the time, Pallas kernels for 4%

profile of v1, /device:TPU:1, one launch (start us, length us, event | category | flops | bytes accessed | tf_op | source)
XLA Modules:
  0.0 111.8 jit_solution(13883611582236399759)
XLA Ops:
  0.6 0.0 copy-start
  0.6 1.0 copy-done
  1.6 0.0 copy-start.1
  1.6 0.9 copy-done.1
  2.6 0.0 copy-start.2
  2.6 0.9 copy-done.2
  3.5 0.0 copy-start.3
  3.5 0.8 copy-done.3
  4.3 0.0 copy-start.4
  4.3 0.8 copy-done.4
  5.2 0.0 copy-start.5
  5.2 0.8 copy-done.5
  6.0 0.0 copy-start.6
  6.0 0.7 copy-done.6
  6.7 17.4 %shard_map.127 = (bf16[5120,128]{1,0:T(8,128)(2,1)S(1)}, f32[768,128]{1,0:T(8,128)S(1)}) custom-call(s32[4,8,128]{2,1,0:T(8,128)S(1)} %bitcast.19, s32[16,768]{1,0:T(8,128)S(1)} %bitcast.18, bf16[768,128]{1,0:T(8,128)(2,1)S(1)} %copy-done.1, bf16[768,256]{1,0:T(8,128)(2,1)S(1)} %copy-done, bf16[768,128]{1,0:T(8,128)(2,1)S(1)} %copy-done.2, ...), custom_call_target="tpu_custom_call" | custom-call | flops 1157627904 | bytes 1310720 | tf_op jit(solution)/shard_map/pallas_call | solution.py:195
  24.0 59.7 %all_to_all.10 = bf16[512,5,2,128]{3,2,1,0:T(2,128)(2,1)S(1)} all-to-all(bf16[512,5,2,128]{3,2,1,0:T(2,128)(2,1)S(1)} %bitcast.16), channel_id=1, replica_groups=mesh['nodes'=128,'grp'=4] {'nodes','grp'}, dimensions={0} | all-to-all | bytes 2621440 | tf_op jit(solution)/shard_map/all_to_all | solution.py:216
  83.7 0.0 copy-start.7
  83.7 1.1 shard_map.129
  84.9 9.7 %all-to-all-start.1 = ((bf16[512,1,2,128]{3,2,1,0:T(2,128)(2,1)}), bf16[512,1,2,128]{3,2,1,0:T(2,128)(2,1)S(1)}, u32[]{:S(2)}, u32[]{:S(2)}) async-start(bf16[512,1,2,128]{3,2,1,0:T(2,128)(2,1)} %bitcast.7), calls=%async_computation.1 | async-start | bytes 524288 | tf_op jit(solution)/shard_map/all_to_all | solution.py:216
  94.5 0.0 copy-done.7
  94.5 0.1 copy.18
  94.7 0.3 reshape.27.recv_ref
  95.0 4.0 %shard_map.128 = bf16[768,128]{1,0:T(8,128)(2,1)} custom-call(s32[40,128]{1,0:T(8,128)S(1)} %reshape.27.recv_ref, bf16[5120,128]{1,0:T(8,128)(2,1)S(1)} %bitcast.15, f32[768,128]{1,0:T(8,128)S(1)} %get-tuple-element.14.total_ref), custom_call_target="tpu_custom_call" | custom-call | flops 1006632960 | bytes 1310720 | tf_op jit(solution)/shard_map/pallas_call | solution.py:227
  99.0 12.0 %all-to-all-done.1 = bf16[512,1,2,128]{3,2,1,0:T(2,128)(2,1)S(1)} async-done(((bf16[512,1,2,128]{3,2,1,0:T(2,128)(2,1)}), bf16[512,1,2,128]{3,2,1,0:T(2,128)(2,1)S(1)}, u32[]{:S(2)}, u32[]{:S(2)}) %all-to-all-start.1) | async-done | bytes 262176 | tf_op jit(solution)/shard_map/all_to_all | solution.py:216
  111.0 0.8 shard_map.130
  (1 shorter events, 0.0 us)
Async XLA Ops:
  0.6 1.0 copy-start
  1.6 0.9 copy-start.1
  2.6 0.9 copy-start.2
  3.5 0.8 copy-start.3
  4.3 0.8 copy-start.4
  5.2 0.8 copy-start.5
  6.0 0.7 copy-start.6
  83.7 10.8 %copy-start.7 = (s32[1,1,128,4,8]{2,4,3,1,0:T(8,128)S(1)}, s32[1,1,128,4,8]{2,4,3,1,0:T(8,128)}, u32[]{:S(2)}) copy-start(s32[1,1,128,4,8]{2,4,3,1,0:T(8,128)} %param.15) | copy-start | bytes 49156
  84.9 26.1 %all-to-all-start.1 = ((bf16[512,1,2,128]{3,2,1,0:T(2,128)(2,1)}), bf16[512,1,2,128]{3,2,1,0:T(2,128)(2,1)S(1)}, u32[]{:S(2)}, u32[]{:S(2)}) async-start(bf16[512,1,2,128]{3,2,1,0:T(2,128)(2,1)} %bitcast.7), calls=%async_computation.1 | async-start | bytes 524288 | tf_op jit(solution)/shard_map/all_to_all | solution.py:216

commit v2 on v1

v2 whole, which is shorter than its diff:
```python
import functools

import jax
import jax.numpy as jnp
from jax import lax
from jax.experimental import pallas as pl
from jax.experimental.pallas import tpu as pltpu
from jax.sharding import PartitionSpec as P

BF16 = jnp.bfloat16
F32 = jnp.float32
PLAIN = (((1,), (0,)), ((), ()))
LAST = (((1,), (1,)), ((), ()))
FIRST = (((0,), (0,)), ((), ()))
LANES = 128
EXTRA = 2
AXES = ("nodes", "grp")


def dot(a, b, dims=PLAIN):
    return lax.dot_general(a, b, dims, preferred_element_type=F32)


def iota(shape, dim):
    return lax.broadcasted_iota(jnp.int32, shape, dim)


def match(a, b):
    shape = jnp.broadcast_shapes(a.shape, b.shape)
    return jnp.where(a == b, jnp.ones(shape, BF16), jnp.zeros(shape, BF16))


def low_part(value):
    return value - value.astype(BF16).astype(F32)


def columns(row):
    return jnp.broadcast_to(row, (LANES, LANES)).T


def remainders(wide, thin):
    lane = iota(wide.shape, 1)
    low = jnp.where(lane == LANES - 2, thin, low_part(wide))
    return jnp.where(lane == LANES - 1, low_part(thin), low).astype(BF16)


def first_kernel(
    send_hbm, lists_hbm, out_hbm, hid_hbm, saved_hbm, w1_hbm, w2_hbm,
    piece_ref, agg_ref, wire_ref,
    send_ref, lists_ref, out_ref, hid_ref, saved_ref, w1_ref, w2_ref, sems,
    high_ref, low_ref, sent_ref, rows_ref, chosen_ref,
):
    groups, slots, nodes = send_ref.shape
    rows = out_ref.shape[0]
    piece = slots + EXTRA
    pairs = [
        (out_hbm, out_ref), (w2_hbm, w2_ref), (hid_hbm, hid_ref), (w1_hbm, w1_ref),
        (saved_hbm, saved_ref), (lists_hbm, lists_ref), (send_hbm, send_ref),
    ]
    copies = [pltpu.make_async_copy(a, b, sems.at[i]) for i, (a, b) in enumerate(pairs)]
    for copy in copies:
        copy.start()

    block = LANES * piece
    lane = iota((block, 2 * LANES), 1)
    chosen_ref[:, rows:] = jnp.where(
        iota(lane.shape, 0) == piece * (lane & (LANES - 1)) + slots + (lane >> 7), 1.0, 0.0
    ).astype(BF16)

    for copy in copies[:4]:
        copy.wait()
    out = out_ref[...]
    hidden = hid_ref[...]
    grad_hidden = dot(out, w2_ref[...], LAST)
    grad_z = jnp.where(hidden > 0, grad_hidden, 0.0).astype(BF16)
    grad_agg = dot(grad_z, w1_ref[...], LAST)
    wire = grad_agg.astype(BF16)
    agg_ref[...] = grad_agg
    wire_ref[...] = wire
    rows_ref[:rows, :] = wire
    for copy in copies[4:]:
        copy.wait()

    low_row = iota((LANES, 1), 0).astype(jnp.int16)
    high_row = iota((16, 1), 0).astype(jnp.int16)
    count = jnp.zeros((LANES, 16), F32)
    for ref in [lists_ref] + [send_ref.at[g] for g in range(groups)]:
        index = ref[...]
        low = (index & (LANES - 1)).astype(jnp.int16)
        high = (index >> 7).astype(jnp.int16)
        for k in range(index.shape[0]):
            count += dot(match(low[k : k + 1], low_row), match(high[k : k + 1], high_row), LAST)
    node = jnp.sum(grad_agg, axis=0, keepdims=True)
    for h in range(rows // LANES):
        carried = wire[h * LANES : (h + 1) * LANES].astype(F32) * count[:, h : h + 1]
        node += jnp.sum(carried, axis=0, keepdims=True)

    part_w1 = dot(saved_ref[...], grad_z, FIRST)
    part_w2 = dot(out, hidden, FIRST)
    sum_z = jnp.sum(grad_z.astype(F32), axis=0, keepdims=True)
    sum_out = jnp.sum(out.astype(F32), axis=0, keepdims=True)
    quarters = [
        (part_w1[:, :LANES], sum_z[:, :LANES]),
        (part_w1[:, LANES:], sum_z[:, LANES:]),
        (part_w2[:, :LANES], sum_out),
        (part_w2[:, LANES:], node),
    ]
    for q, (wide, thin) in enumerate(quarters):
        high_ref[q * LANES : (q + 1) * LANES, :] = wide.astype(BF16)
        low_ref[q * LANES : (q + 1) * LANES, :] = remainders(wide, columns(thin))

    parts = []
    for g in range(groups):
        parts += [send_ref[g], jnp.full((EXTRA, nodes), rows, jnp.int32)]
    sent = jnp.concatenate(parts, axis=0)
    sent_ref[...] = jnp.concatenate([sent, pltpu.roll(sent, nodes - 1, 1)], axis=0)
    lane_index = iota((16, rows), 1).astype(jnp.int16)
    width = LANES // groups

    @pl.loop(0, nodes // width)
    def _(step):
        own = pl.ds(pl.multiple_of(step * LANES, LANES), LANES)
        rows_ref[rows : rows + LANES, :] = high_ref[own, :]
        rows_ref[rows + LANES :, :] = low_ref[own, :]
        sent = pltpu.roll(sent_ref[...], nodes - step * width, 1).astype(jnp.int16)
        for n in range(0, width, 2):
            for r in range(0, 2 * groups * piece, 16):
                column = jnp.broadcast_to(sent[r : r + 16, n : n + 1], (16, rows))
                start = n * groups * piece + r
                chosen_ref[start : start + 16, :rows] = match(column, lane_index)
        piece_ref[pl.ds(pl.multiple_of(step * block, block), block), :] = dot(
            chosen_ref[...], rows_ref[...]
        ).astype(BF16)


def local_kernel(lists_ref, recv_ref, wire_ref, agg_ref, total_ref, target_ref, counts_ref):
    rows = wire_ref.shape[0]
    row_index = iota((rows, 1), 0).astype(jnp.int16)
    for tile in range(rows // LANES):
        lists = lists_ref[:, tile * LANES : (tile + 1) * LANES].astype(jnp.int16)
        counts = match(lists[0:1], row_index)
        for k in range(1, lists_ref.shape[0]):
            counts += match(lists[k : k + 1], row_index)
        counts_ref[:, tile * LANES : (tile + 1) * LANES] = counts
    local = dot(wire_ref[...].T, counts_ref[...])
    total_ref[...] = agg_ref[...] + local.T
    target_ref[...] = recv_ref[...]


def chunk_kernel(piece, scale, arrived_ref, share_ref):
    span = piece * LANES
    lane = iota((16, span), 1)
    place = lane - piece * ((lane * ((1 << 16) // piece + 1)) >> 16)
    pick = jnp.where(place == piece - EXTRA + iota((16, span), 0), 1.0, 0.0).astype(BF16)
    sums = jnp.zeros((16, LANES), F32)
    for start in range(0, arrived_ref.shape[0], span):
        sums += dot(pick, arrived_ref[start : start + span, :])
    high, low = sums[0:1], sums[1:2]
    lane = iota(high.shape, 1)
    last = jnp.sum(jnp.where(lane >= LANES - 2, low, 0.0), axis=1, keepdims=True)
    wide = scale * (high + jnp.where(lane >= LANES - 2, 0.0, low))
    thin = jnp.broadcast_to(scale * last, wide.shape)
    pair = jnp.concatenate([wide.astype(BF16), remainders(wide, thin)], axis=0)
    share_ref[...] = jnp.concatenate([pair] * (share_ref.shape[0] // EXTRA), axis=0)


def remote_kernel(recv_ref, arrived_ref, total_ref, x_ref):
    rows = total_ref.shape[0]
    row_index = iota((rows, 1), 0).astype(jnp.int16)
    targets = recv_ref[...].astype(jnp.int16)
    total = total_ref[...]
    for r in range(0, recv_ref.shape[0], 2):
        chosen = jnp.concatenate([match(targets[q : q + 1], row_index) for q in (r, r + 1)], axis=1)
        total += dot(chosen, arrived_ref[r * LANES : (r + 2) * LANES, :])
    x_ref[...] = total.astype(BF16)


def last_kernel(share_ref, w1_ref, b1_ref, w2_ref, b2_ref, node_ref, rows_ref):
    rows_ref[...] = share_ref[...].astype(F32)
    half = rows_ref.shape[0] // 2
    high = rows_ref[pl.ds(0, half, 2), :]
    low = rows_ref[pl.ds(1, half, 2), :]
    lane = iota(high.shape, 1)
    wide = high + jnp.where(lane >= LANES - 2, 0.0, low)
    w1_ref[:, :LANES] = wide[:LANES]
    w1_ref[:, LANES:] = wide[LANES : 2 * LANES]
    w2_ref[:LANES, :] = wide[2 * LANES : 3 * LANES].T
    w2_ref[LANES:, :] = wide[3 * LANES :].T
    thin = []
    for q in range(4):
        turned = low[q * LANES : (q + 1) * LANES].T
        thin.append(turned[LANES - 2 : LANES - 1] + turned[LANES - 1 :])
    b1_ref[...] = jnp.concatenate(thin[:2], axis=1)
    b2_ref[...] = thin[2]
    node_ref[...] = thin[3]


def call(kernel, outs, scratch=(), hbm=0, limit=24, **cost):
    specs = {"in_specs": [pl.BlockSpec(memory_space=pltpu.HBM)] * hbm} if hbm else {}
    return pl.pallas_call(
        kernel,
        out_shape=[jax.ShapeDtypeStruct(shape, dtype) for shape, dtype in outs],
        scratch_shapes=list(scratch),
        compiler_params=pltpu.CompilerParams(vmem_limit_bytes=limit << 20),
        cost_estimate=pl.CostEstimate(transcendentals=0, **cost),
        **specs,
    )


def per_device(
    grad_out, agg_saved, hidden_saved, w_one, w_two, local_lists, send_slots, receive_slots
):
    rows, width = grad_out.shape
    hidden = hidden_saved.shape[1]
    nodes, groups, slots = send_slots.shape[2:]
    devices = nodes * groups
    piece = slots + EXTRA
    lists = local_lists.T
    sources = [jnp.transpose(send_slots[0, 0], (1, 2, 0)), lists, grad_out, hidden_saved, agg_saved, w_one, w_two]
    pieces, agg, wire = call(
        first_kernel,
        [((devices * piece, width), BF16), ((rows, width), F32), ((rows, width), BF16)],
        [pltpu.VMEM(x.shape, x.dtype) for x in sources]
        + [
            pltpu.SemaphoreType.DMA((len(sources),)),
            pltpu.VMEM((devices, LANES), BF16),
            pltpu.VMEM((devices, LANES), BF16),
            pltpu.VMEM((2 * groups * piece, nodes), jnp.int32),
            pltpu.VMEM((rows + 2 * LANES, width), BF16),
            pltpu.VMEM((LANES * piece, rows + 2 * LANES), BF16),
        ],
        hbm=len(sources),
        limit=60,
        flops=2 * devices * piece * rows * width,
        bytes_accessed=devices * piece * width * 2,
    )(*sources)
    recv = jnp.pad(receive_slots[0, 0], ((0, 0), (0, 0), (0, EXTRA)), constant_values=rows)
    total, targets = call(
        local_kernel,
        [((rows, width), F32), ((devices * piece // LANES, LANES), jnp.int32)],
        [pltpu.VMEM((rows, rows), BF16)],
        flops=2 * rows * rows * width,
        bytes_accessed=rows * width * 10,
    )(lists, recv.reshape(-1, LANES), wire, agg)

    def exchange(x, height):
        x = x.reshape(devices, height // 2, 2, width)
        return lax.all_to_all(x, AXES, split_axis=0, concat_axis=0, tiled=True).reshape(-1, width)

    arrived = exchange(pieces, piece)
    (share,) = call(
        functools.partial(chunk_kernel, piece, 1.0 / devices),
        [((devices * EXTRA, width), BF16)],
        flops=2 * 16 * devices * piece * width,
        bytes_accessed=devices * piece * width * 2,
    )(arrived)
    shares = exchange(share, EXTRA)
    (grad_x,) = call(
        remote_kernel,
        [((rows, width), BF16)],
        flops=2 * devices * piece * rows * width,
        bytes_accessed=devices * piece * width * 2,
    )(targets, arrived, total)
    w1, b1, w2, b2, node = call(
        last_kernel,
        [
            ((width, hidden), F32),
            ((1, hidden), F32),
            ((hidden, width), F32),
            ((1, width), F32),
            ((1, width), F32),
        ],
        [pltpu.VMEM((devices * EXTRA, width), F32)],
        flops=0,
        bytes_accessed=devices * EXTRA * width * 2,
    )(shares)
    return grad_x, w1, b1[0], w2, b2[0], node[0]


def solution(mesh):
    placed = (
        P(AXES, None),
        P(AXES, None),
        P(AXES, None),
        P(),
        P(),
        P(AXES, None),
        P("nodes", "grp", None, None, None),
        P("nodes", "grp", None, None, None),
    )
    return jax.shard_map(
        per_device,
        mesh=mesh,
        in_specs=placed,
        out_specs=(P(AXES, None), P(), P(), P(), P(), P()),
        check_vma=False,
    )
```

time: 112 us -> 97.8 us (0.87)
  Pallas kernels: 23.3 us -> 16.2 us
  local copies, waits for them, and re-layouts: 6.51 us -> 0.48 us
  waiting for transfers between devices: 12 us -> 10.6 us
    pallas_call x1, Pallas kernels: 17.4 us -> 9 us  [per_device(): call(first_kernel, [((devices * piece, width), BF16), ((rows, width), F32...]
    unnamed x17 -> x9, local copies, waits for them, and re-layouts: 6.18 us -> 0.16 us
    pallas_call x0 -> x1, Pallas kernels: none -> 2.4 us  [per_device(): call(local_kernel, [((rows, width), F32), ((devices * piece // LANES, LAN...]
    all_to_all x1, waiting for transfers between devices: 12 us -> 10.6 us  [exchange(): lax.all_to_all(x, AXES, split_axis=0, concat_axis=0, tiled=True)]
  transfers between devices with their start and end apart: 1 -> 1, of which waited for: 1 -> 1; matrix products, arithmetic and copies ran while one was open for 0% -> 0% of each run, Pallas kernels for 4% -> 5%
where the time goes in v2:
time: 97.8 us; the launch traced here: 97.6 us
  blocking collectives  59.9 us (61%)
  Pallas kernels  16.2 us (17%)
  waiting for transfers between devices  10.6 us (11%)
  starting transfers between devices  9.67 us (10%)
    all_to_all x1, blocking collectives, exchange(): lax.all_to_all(x, AXES, split_axis=0, concat_axis=0, tiled=True)  59.9 us
    all_to_all x1, waiting for transfers between devices, exchange(): lax.all_to_all(x, AXES, split_axis=0, concat_axis=0, tiled=True)  10.6 us
    all_to_all x1, starting transfers between devices, exchange(): lax.all_to_all(x, AXES, split_axis=0, concat_axis=0, tiled=True)  9.67 us
    pallas_call x1, Pallas kernels, per_device(): call(first_kernel, [((devices * piece, width), BF16), ((rows, width), F32...  9 us
    pallas_call x1, Pallas kernels, per_device(): call(remote_kernel, [((rows, width), BF16)], flops=2 * devices * piece *...  2.87 us
    pallas_call x1, Pallas kernels, per_device(): call(local_kernel, [((rows, width), F32), ((devices * piece // LANES, LAN...  2.4 us
  transfers between devices with their start and end apart: 1, of which 1 were waited for; matrix products, arithmetic and copies ran while one was open for 0% of the time, Pallas kernels for 5%

profile of v2, /device:TPU:1, one launch (start us, length us, event | category | flops | bytes accessed | tf_op | source)
XLA Modules:
  0.0 97.6 jit_solution(16070901238572844673)
XLA Ops:
  0.6 9.0 %shard_map.127 = (bf16[5120,128]{1,0:T(8,128)(2,1)}, f32[768,128]{1,0:T(8,128)}, bf16[768,128]{1,0:T(8,128)(2,1)}) custom-call(s32[4,8,128]{2,1,0:T(8,128)} %bitcast.21, s32[16,768]{1,0:T(8,128)} %bitcast.17, bf16[768,128]{1,0:T(8,128)(2,1)} %out_hbm.1, bf16[768,256]{1,0:T(8,128)(2,1)} %hid_hbm.1, bf16[768,128]{1,0:T(8,128)(2,1)} %saved_hbm.1, ...), custom_call_target="tpu_custom_call" | custom-call | flops 1006632960 | bytes 1310720 | tf_op jit(solution)/shard_map/pallas_call | solution.py:220
  9.6 59.9 %all_to_all.10 = bf16[512,5,2,128]{3,2,1,0:T(2,128)(2,1)S(1)} all-to-all(bf16[512,5,2,128]{3,2,1,0:T(2,128)(2,1)} %bitcast.19), channel_id=1, replica_groups=mesh['nodes'=128,'grp'=4] {'nodes','grp'}, dimensions={0} | all-to-all | bytes 2621440 | tf_op jit(solution)/shard_map/all_to_all | solution.py:248
  69.5 0.0 copy-start.3
  69.5 0.0 copy-start
  69.5 0.0 copy-start.1
  69.5 0.0 copy-start.2
  69.6 1.1 %shard_map.130 = bf16[1024,128]{1,0:T(8,128)(2,1)} custom-call(bf16[5120,128]{1,0:T(8,128)(2,1)S(1)} %bitcast.14), custom_call_target="tpu_custom_call" | custom-call | flops 20971520 | bytes 1310720 | tf_op jit(solution)/shard_map/pallas_call | solution.py:251
  70.7 9.7 %all-to-all-start.1 = ((bf16[512,1,2,128]{3,2,1,0:T(2,128)(2,1)}), bf16[512,1,2,128]{3,2,1,0:T(2,128)(2,1)S(1)}, u32[]{:S(2)}, u32[]{:S(2)}) async-start(bf16[512,1,2,128]{3,2,1,0:T(2,128)(2,1)} %bitcast.7), calls=%async_computation.1 | async-start | bytes 524288 | tf_op jit(solution)/shard_map/all_to_all | solution.py:248
  80.3 0.0 copy-done.3
  80.3 0.1 copy.18
  80.6 0.3 reshape.27.recv_ref
  80.8 0.0 copy-done
  80.8 0.0 copy-done.1
  80.9 0.0 copy-done.2
  80.9 2.4 %shard_map.128 = (f32[768,128]{1,0:T(8,128)S(1)}, s32[40,128]{1,0:T(8,128)S(1)}) custom-call(s32[16,768]{1,0:T(8,128)S(1)} %bitcast.18, s32[40,128]{1,0:T(8,128)S(1)} %reshape.27.recv_ref, bf16[768,128]{1,0:T(8,128)(2,1)S(1)} %copy-done.1, f32[768,128]{1,0:T(8,128)S(1)} %copy-done), custom_call_target="tpu_custom_call" | custom-call | flops 150994944 | bytes 983040 | tf_op jit(solution)/shard_map/pallas_call | solution.py:238
  83.3 2.9 %shard_map.129 = bf16[768,128]{1,0:T(8,128)(2,1)} custom-call(s32[40,128]{1,0:T(8,128)S(1)} %get-tuple-element.18.recv_ref, bf16[5120,128]{1,0:T(8,128)(2,1)S(1)} %bitcast.15, f32[768,128]{1,0:T(8,128)S(1)} %get-tuple-element.20.total_ref), custom_call_target="tpu_custom_call" | custom-call | flops 1006632960 | bytes 1310720 | tf_op jit(solution)/shard_map/pallas_call | solution.py:258
  86.1 10.6 %all-to-all-done.1 = bf16[512,1,2,128]{3,2,1,0:T(2,128)(2,1)S(1)} async-done(((bf16[512,1,2,128]{3,2,1,0:T(2,128)(2,1)}), bf16[512,1,2,128]{3,2,1,0:T(2,128)(2,1)S(1)}, u32[]{:S(2)}, u32[]{:S(2)}) %all-to-all-start.1) | async-done | bytes 262176 | tf_op jit(solution)/shard_map/all_to_all | solution.py:248
  96.8 0.8 shard_map.131
  (1 shorter events, 0.0 us)
Async XLA Ops:
  69.5 10.8 %copy-start.3 = (s32[1,1,128,4,8]{2,4,3,1,0:T(8,128)S(1)}, s32[1,1,128,4,8]{2,4,3,1,0:T(8,128)}, u32[]{:S(2)}) copy-start(s32[1,1,128,4,8]{2,4,3,1,0:T(8,128)} %param.15) | copy-start | bytes 49156
  69.5 11.3 %copy-start = (f32[768,128]{1,0:T(8,128)S(1)}, f32[768,128]{1,0:T(8,128)}, u32[]{:S(2)}) copy-start(f32[768,128]{1,0:T(8,128)} %get-tuple-element.17.agg_ref) | copy-start | bytes 1179652
  69.5 11.3 %copy-start.1 = (bf16[768,128]{1,0:T(8,128)(2,1)S(1)}, bf16[768,128]{1,0:T(8,128)(2,1)}, u32[]{:S(2)}) copy-start(bf16[768,128]{1,0:T(8,128)(2,1)} %get-tuple-element.16.wire_ref) | copy-start | bytes 589828
  69.5 11.3 %copy-start.2 = (s32[768,16]{0,1:T(8,128)S(1)}, s32[768,16]{0,1:T(8,128)}, u32[]{:S(2)}) copy-start(s32[768,16]{0,1:T(8,128)} %param.13) | copy-start | bytes 147460
  70.7 26.1 %all-to-all-start.1 = ((bf16[512,1,2,128]{3,2,1,0:T(2,128)(2,1)}), bf16[512,1,2,128]{3,2,1,0:T(2,128)(2,1)S(1)}, u32[]{:S(2)}, u32[]{:S(2)}) async-start(bf16[512,1,2,128]{3,2,1,0:T(2,128)(2,1)} %bitcast.7), calls=%async_computation.1 | async-start | bytes 524288 | tf_op jit(solution)/shard_map/all_to_all | solution.py:248

commit v3 on v2

--- a/solution.py
+++ b/solution.py
@@ -45,29 +45,51 @@
 
 
 def first_kernel(
-    send_hbm, lists_hbm, out_hbm, hid_hbm, saved_hbm, w1_hbm, w2_hbm,
-    piece_ref, agg_ref, wire_ref,
-    send_ref, lists_ref, out_ref, hid_ref, saved_ref, w1_ref, w2_ref, sems,
-    high_ref, low_ref, sent_ref, rows_ref, chosen_ref,
+    send_hbm, out_hbm, w2_hbm, hid_hbm, w1_hbm, lists_hbm, saved_hbm,
+    piece_hbm, agg_hbm, wire_hbm,
+    send_ref, out_ref, w2_ref, hid_ref, w1_ref, lists_ref, saved_ref, in_sems,
+    piece_ref, agg_ref, wire_ref, out_sems,
+    rows_ref, chosen_ref,
 ):
     groups, slots, nodes = send_ref.shape
     rows = out_ref.shape[0]
     piece = slots + EXTRA
+    block = LANES * piece
+    width = LANES // groups
+    blocks = nodes // width
     pairs = [
-        (out_hbm, out_ref), (w2_hbm, w2_ref), (hid_hbm, hid_ref), (w1_hbm, w1_ref),
-        (saved_hbm, saved_ref), (lists_hbm, lists_ref), (send_hbm, send_ref),
+        (send_hbm, send_ref), (out_hbm, out_ref), (w2_hbm, w2_ref), (hid_hbm, hid_ref),
+        (w1_hbm, w1_ref), (lists_hbm, lists_ref), (saved_hbm, saved_ref),
     ]
-    copies = [pltpu.make_async_copy(a, b, sems.at[i]) for i, (a, b) in enumerate(pairs)]
-    for copy in copies:
+    arrivals = [pltpu.make_async_copy(a, b, in_sems.at[i]) for i, (a, b) in enumerate(pairs)]
+    for copy in arrivals:
         copy.start()
 
-    block = LANES * piece
     lane = iota((block, 2 * LANES), 1)
-    chosen_ref[:, rows:] = jnp.where(
+    place = jnp.where(
         iota(lane.shape, 0) == piece * (lane & (LANES - 1)) + slots + (lane >> 7), 1.0, 0.0
     ).astype(BF16)
-
-    for copy in copies[:4]:
+    for step in range(blocks):
+        chosen_ref[step, :, rows:] = place
+
+    arrivals[0].wait()
+    parts = []
+    for g in range(groups):
+        parts += [send_ref[g], jnp.full((EXTRA, nodes), rows, jnp.int32)]
+    sent = jnp.concatenate(parts, axis=0)
+    sent = jnp.concatenate([sent, pltpu.roll(sent, nodes - 1, 1)], axis=0).astype(jnp.int16)
+    lane_index = iota((16, rows), 1).astype(jnp.int16)
+
+    def choose(step):
+        for n in range(0, width, 2):
+            for r in range(0, 2 * groups * piece, 16):
+                at = step * width + n
+                column = jnp.broadcast_to(sent[r : r + 16, at : at + 1], (16, rows))
+                start = n * groups * piece + r
+                chosen_ref[step, start : start + 16, :rows] = match(column, lane_index)
+
+    choose(0)
+    for copy in arrivals[1:5]:
         copy.wait()
     out = out_ref[...]
     hidden = hid_ref[...]
@@ -77,8 +99,15 @@
     wire = grad_agg.astype(BF16)
     agg_ref[...] = grad_agg
     wire_ref[...] = wire
-    rows_ref[:rows, :] = wire
-    for copy in copies[4:]:
+    departures = [
+        pltpu.make_async_copy(agg_ref, agg_hbm, out_sems.at[0]),
+        pltpu.make_async_copy(wire_ref, wire_hbm, out_sems.at[1]),
+    ]
+    for copy in departures:
+        copy.start()
+    for step in range(blocks):
+        rows_ref[step, :rows, :] = wire
+    for copy in arrivals[5:]:
         copy.wait()
 
     low_row = iota((LANES, 1), 0).astype(jnp.int16)
@@ -105,32 +134,19 @@
         (part_w2[:, :LANES], sum_out),
         (part_w2[:, LANES:], node),
     ]
-    for q, (wide, thin) in enumerate(quarters):
-        high_ref[q * LANES : (q + 1) * LANES, :] = wide.astype(BF16)
-        low_ref[q * LANES : (q + 1) * LANES, :] = remainders(wide, columns(thin))
-
-    parts = []
-    for g in range(groups):
-        parts += [send_ref[g], jnp.full((EXTRA, nodes), rows, jnp.int32)]
-    sent = jnp.concatenate(parts, axis=0)
-    sent_ref[...] = jnp.concatenate([sent, pltpu.roll(sent, nodes - 1, 1)], axis=0)
-    lane_index = iota((16, rows), 1).astype(jnp.int16)
-    width = LANES // groups
-
-    @pl.loop(0, nodes // width)
-    def _(step):
-        own = pl.ds(pl.multiple_of(step * LANES, LANES), LANES)
-        rows_ref[rows : rows + LANES, :] = high_ref[own, :]
-        rows_ref[rows + LANES :, :] = low_ref[own, :]
-        sent = pltpu.roll(sent_ref[...], nodes - step * width, 1).astype(jnp.int16)
-        for n in range(0, width, 2):
-            for r in range(0, 2 * groups * piece, 16):
-                column = jnp.broadcast_to(sent[r : r + 16, n : n + 1], (16, rows))
-                start = n * groups * piece + r
-                chosen_ref[start : start + 16, :rows] = match(column, lane_index)
-        piece_ref[pl.ds(pl.multiple_of(step * block, block), block), :] = dot(
-            chosen_ref[...], rows_ref[...]
-        ).astype(BF16)
+
+    for step, (wide, thin) in enumerate(quarters):
+        if step:
+            choose(step)
+        rows_ref[step, rows : rows + LANES, :] = wide.astype(BF16)
+        rows_ref[step, rows + LANES :, :] = remainders(wide, columns(thin))
+        own = pl.ds(step * block, block)
+        piece_ref[own, :] = dot(chosen_ref[step], rows_ref[step]).astype(BF16)
+        copy = pltpu.make_async_copy(piece_ref.at[own], piece_hbm.at[own], out_sems.at[2 + step])
+        copy.start()
+        departures.append(copy)
+    for copy in departures:
+        copy.wait()
 
 
 def local_kernel(lists_ref, recv_ref, wire_ref, agg_ref, total_ref, target_ref, counts_ref):
@@ -195,8 +211,9 @@
     node_ref[...] = thin[3]
 
 
-def call(kernel, outs, scratch=(), hbm=0, limit=24, **cost):
-    specs = {"in_specs": [pl.BlockSpec(memory_space=pltpu.HBM)] * hbm} if hbm else {}
+def call(kernel, outs, scratch=(), far=0, limit=24, **cost):
+    hbm = pl.BlockSpec(memory_space=pltpu.HBM)
+    specs = {"in_specs": [hbm] * far, "out_specs": [hbm] * len(outs)} if far else {}
     return pl.pallas_call(
         kernel,
         out_shape=[jax.ShapeDtypeStruct(shape, dtype) for shape, dtype in outs],
@@ -216,20 +233,22 @@
     devices = nodes * groups
     piece = slots + EXTRA
     lists = local_lists.T
-    sources = [jnp.transpose(send_slots[0, 0], (1, 2, 0)), lists, grad_out, hidden_saved, agg_saved, w_one, w_two]
+    send = jnp.transpose(send_slots[0, 0], (1, 2, 0))
+    sources = [send, grad_out, w_two, hidden_saved, w_one, lists, agg_saved]
+    outs = [((devices * piece, width), BF16), ((rows, width), F32), ((rows, width), BF16)]
+    blocks = devices // LANES
     pieces, agg, wire = call(
         first_kernel,
-        [((devices * piece, width), BF16), ((rows, width), F32), ((rows, width), BF16)],
+        outs,
         [pltpu.VMEM(x.shape, x.dtype) for x in sources]
+        + [pltpu.SemaphoreType.DMA((len(sources),))]
+        + [pltpu.VMEM(*out) for out in outs]
         + [
-            pltpu.SemaphoreType.DMA((len(sources),)),
-            pltpu.VMEM((devices, LANES), BF16),
-            pltpu.VMEM((devices, LANES), BF16),
-            pltpu.VMEM((2 * groups * piece, nodes), jnp.int32),
-            pltpu.VMEM((rows + 2 * LANES, width), BF16),
-            pltpu.VMEM((LANES * piece, rows + 2 * LANES), BF16),
+            pltpu.SemaphoreType.DMA((2 + blocks,)),
+            pltpu.VMEM((blocks, rows + 2 * LANES, width), BF16),
+            pltpu.VMEM((blocks, LANES * piece, rows + 2 * LANES), BF16),
         ],
-        hbm=len(sources),
+        far=len(sources),
         limit=60,
         flops=2 * devices * piece * rows * width,
         bytes_accessed=devices * piece * width * 2,

time: 97.8 us -> 95.6 us (0.978)
  Pallas kernels: 16.2 us -> 13.9 us
    pallas_call x1, Pallas kernels: 9 us -> 6.72 us  [per_device(): call(first_kernel, outs, [pltpu.VMEM(x.shape, x.dtype) for x in sources]...]
  transfers between devices with their start and end apart: 1 -> 1, of which waited for: 1 -> 1; matrix products, arithmetic and copies ran while one was open for 0% -> 0% of each run, Pallas kernels for 5% -> 6%
where the time goes in v3:
time: 95.6 us; the launch traced here: 95.3 us
  blocking collectives  59.9 us (63%)
  Pallas kernels  13.9 us (15%)
  waiting for transfers between devices  10.6 us (11%)
  starting transfers between devices  9.67 us (10%)
    all_to_all x1, blocking collectives, exchange(): lax.all_to_all(x, AXES, split_axis=0, concat_axis=0, tiled=True)  59.9 us
    all_to_all x1, waiting for transfers between devices, exchange(): lax.all_to_all(x, AXES, split_axis=0, concat_axis=0, tiled=True)  10.6 us
    all_to_all x1, starting transfers between devices, exchange(): lax.all_to_all(x, AXES, split_axis=0, concat_axis=0, tiled=True)  9.67 us
    pallas_call x1, Pallas kernels, per_device(): call(first_kernel, outs, [pltpu.VMEM(x.shape, x.dtype) for x in sources]...  6.72 us
    pallas_call x1, Pallas kernels, per_device(): call(remote_kernel, [((rows, width), BF16)], flops=2 * devices * piece *...  2.87 us
    pallas_call x1, Pallas kernels, per_device(): call(local_kernel, [((rows, width), F32), ((devices * piece // LANES, LAN...  2.4 us
  transfers between devices with their start and end apart: 1, of which 1 were waited for; matrix products, arithmetic and copies ran while one was open for 0% of the time, Pallas kernels for 6%

profile of v3, /device:TPU:1, one launch (start us, length us, event | category | flops | bytes accessed | tf_op | source)
XLA Modules:
  0.0 95.3 jit_solution(16509022761106959514)
XLA Ops:
  0.6 6.7 %shard_map.127 = (bf16[5120,128]{1,0:T(8,128)(2,1)}, f32[768,128]{1,0:T(8,128)}, bf16[768,128]{1,0:T(8,128)(2,1)}) custom-call(s32[4,8,128]{2,1,0:T(8,128)} %bitcast.21, bf16[768,128]{1,0:T(8,128)(2,1)} %out_hbm.1, bf16[256,128]{1,0:T(8,128)(2,1)} %w2_hbm.1, bf16[768,256]{1,0:T(8,128)(2,1)} %hid_hbm.1, bf16[128,256]{1,0:T(8,128)(2,1)} %w1_hbm.1, ...), custom_call_target="tpu_custom_call" | custom-call | flops 1006632960 | bytes 1310720 | tf_op jit(solution)/shard_map/pallas_call | solution.py:240
  7.4 59.9 %all_to_all.10 = bf16[512,5,2,128]{3,2,1,0:T(2,128)(2,1)S(1)} all-to-all(bf16[512,5,2,128]{3,2,1,0:T(2,128)(2,1)} %bitcast.19), channel_id=1, replica_groups=mesh['nodes'=128,'grp'=4] {'nodes','grp'}, dimensions={0} | all-to-all | bytes 2621440 | tf_op jit(solution)/shard_map/all_to_all | solution.py:267
  67.3 0.0 copy-start.3
  67.3 0.0 copy-start
  67.3 0.0 copy-start.1
  67.3 0.0 copy-start.2
  67.3 1.1 %shard_map.130 = bf16[1024,128]{1,0:T(8,128)(2,1)} custom-call(bf16[5120,128]{1,0:T(8,128)(2,1)S(1)} %bitcast.14), custom_call_target="tpu_custom_call" | custom-call | flops 20971520 | bytes 1310720 | tf_op jit(solution)/shard_map/pallas_call | solution.py:270
  68.4 9.7 %all-to-all-start.1 = ((bf16[512,1,2,128]{3,2,1,0:T(2,128)(2,1)}), bf16[512,1,2,128]{3,2,1,0:T(2,128)(2,1)S(1)}, u32[]{:S(2)}, u32[]{:S(2)}) async-start(bf16[512,1,2,128]{3,2,1,0:T(2,128)(2,1)} %bitcast.7), calls=%async_computation.1 | async-start | bytes 524288 | tf_op jit(solution)/shard_map/all_to_all | solution.py:267
  78.1 0.0 copy-done.3
  78.1 0.1 copy.18
  78.3 0.3 reshape.27.recv_ref
  78.6 0.0 copy-done
  78.6 0.0 copy-done.1
  78.6 0.0 copy-done.2
  78.6 2.4 %shard_map.128 = (f32[768,128]{1,0:T(8,128)S(1)}, s32[40,128]{1,0:T(8,128)S(1)}) custom-call(s32[16,768]{1,0:T(8,128)S(1)} %bitcast.18, s32[40,128]{1,0:T(8,128)S(1)} %reshape.27.recv_ref, bf16[768,128]{1,0:T(8,128)(2,1)S(1)} %copy-done.1, f32[768,128]{1,0:T(8,128)S(1)} %copy-done), custom_call_target="tpu_custom_call" | custom-call | flops 150994944 | bytes 983040 | tf_op jit(solution)/shard_map/pallas_call | solution.py:257
  81.0 2.9 %shard_map.129 = bf16[768,128]{1,0:T(8,128)(2,1)} custom-call(s32[40,128]{1,0:T(8,128)S(1)} %get-tuple-element.18.recv_ref, bf16[5120,128]{1,0:T(8,128)(2,1)S(1)} %bitcast.15, f32[768,128]{1,0:T(8,128)S(1)} %get-tuple-element.20.total_ref), custom_call_target="tpu_custom_call" | custom-call | flops 1006632960 | bytes 1310720 | tf_op jit(solution)/shard_map/pallas_call | solution.py:277
  83.9 10.6 %all-to-all-done.1 = bf16[512,1,2,128]{3,2,1,0:T(2,128)(2,1)S(1)} async-done(((bf16[512,1,2,128]{3,2,1,0:T(2,128)(2,1)}), bf16[512,1,2,128]{3,2,1,0:T(2,128)(2,1)S(1)}, u32[]{:S(2)}, u32[]{:S(2)}) %all-to-all-start.1) | async-done | bytes 262176 | tf_op jit(solution)/shard_map/all_to_all | solution.py:267
  94.5 0.8 shard_map.131
  (1 shorter events, 0.0 us)
Async XLA Ops:
  67.3 10.8 %copy-start.3 = (s32[1,1,128,4,8]{2,4,3,1,0:T(8,128)S(1)}, s32[1,1,128,4,8]{2,4,3,1,0:T(8,128)}, u32[]{:S(2)}) copy-start(s32[1,1,128,4,8]{2,4,3,1,0:T(8,128)} %param.15) | copy-start | bytes 49156
  67.3 11.3 %copy-start = (f32[768,128]{1,0:T(8,128)S(1)}, f32[768,128]{1,0:T(8,128)}, u32[]{:S(2)}) copy-start(f32[768,128]{1,0:T(8,128)} %get-tuple-element.17.agg_ref) | copy-start | bytes 1179652
  67.3 11.3 %copy-start.1 = (bf16[768,128]{1,0:T(8,128)(2,1)S(1)}, bf16[768,128]{1,0:T(8,128)(2,1)}, u32[]{:S(2)}) copy-start(bf16[768,128]{1,0:T(8,128)(2,1)} %get-tuple-element.16.wire_ref) | copy-start | bytes 589828
  67.3 11.3 %copy-start.2 = (s32[768,16]{0,1:T(8,128)S(1)}, s32[768,16]{0,1:T(8,128)}, u32[]{:S(2)}) copy-start(s32[768,16]{0,1:T(8,128)} %param.13) | copy-start | bytes 147460
  68.4 26.1 %all-to-all-start.1 = ((bf16[512,1,2,128]{3,2,1,0:T(2,128)(2,1)}), bf16[512,1,2,128]{3,2,1,0:T(2,128)(2,1)S(1)}, u32[]{:S(2)}, u32[]{:S(2)}) async-start(bf16[512,1,2,128]{3,2,1,0:T(2,128)(2,1)} %bitcast.7), calls=%async_computation.1 | async-start | bytes 524288 | tf_op jit(solution)/shard_map/all_to_all | solution.py:267

commit v4 on v3

--- a/solution.py
+++ b/solution.py
@@ -49,7 +49,7 @@
     piece_hbm, agg_hbm, wire_hbm,
     send_ref, out_ref, w2_ref, hid_ref, w1_ref, lists_ref, saved_ref, in_sems,
     piece_ref, agg_ref, wire_ref, out_sems,
-    rows_ref, chosen_ref,
+    rows_ref, chosen_ref, index_ref,
 ):
     groups, slots, nodes = send_ref.shape
     rows = out_ref.shape[0]
@@ -65,28 +65,32 @@
     for copy in arrivals:
         copy.start()
 
-    lane = iota((block, 2 * LANES), 1)
+    half = rows // 2
     place = jnp.where(
-        iota(lane.shape, 0) == piece * (lane & (LANES - 1)) + slots + (lane >> 7), 1.0, 0.0
-    ).astype(BF16)
+        iota((block, LANES), 0) // piece * piece == piece * iota((block, LANES), 1), 1.0, 0.0
+    )
+    place = jnp.where(iota((block, LANES), 0) % piece >= slots, place, 0.0).astype(BF16)
     for step in range(blocks):
-        chosen_ref[step, :, rows:] = place
+        chosen_ref[step, :, half:] = place
 
     arrivals[0].wait()
     parts = []
     for g in range(groups):
-        parts += [send_ref[g], jnp.full((EXTRA, nodes), rows, jnp.int32)]
+        parts += [send_ref[g], jnp.full((1, nodes), -1, jnp.int32), jnp.full((1, nodes), 2 * rows, jnp.int32)]
     sent = jnp.concatenate(parts, axis=0)
     sent = jnp.concatenate([sent, pltpu.roll(sent, nodes - 1, 1)], axis=0).astype(jnp.int16)
-    lane_index = iota((16, rows), 1).astype(jnp.int16)
+    lane_index = iota((16, half), 1).astype(jnp.int16)
 
     def choose(step):
         for n in range(0, width, 2):
             for r in range(0, 2 * groups * piece, 16):
                 at = step * width + n
-                column = jnp.broadcast_to(sent[r : r + 16, at : at + 1], (16, rows))
                 start = n * groups * piece + r
-                chosen_ref[step, start : start + 16, :rows] = match(column, lane_index)
+                index = jnp.broadcast_to(sent[r : r + 16, at : at + 1], (16, LANES))
+                index_ref[step, start : start + 16, :] = index
+                folded = jnp.where(index >= half, index - half, index)
+                for t in range(0, half, LANES):
+                    chosen_ref[step, start : start + 16, t : t + LANES] = match(folded, lane_index[:, t : t + LANES])
 
     choose(0)
     for copy in arrivals[1:5]:
@@ -106,23 +110,24 @@
     for copy in departures:
         copy.start()
     for step in range(blocks):
-        rows_ref[step, :rows, :] = wire
+        rows_ref[step, :half, :LANES] = wire[:half]
+        rows_ref[step, :half, LANES:] = wire[half:]
     for copy in arrivals[5:]:
         copy.wait()
 
-    low_row = iota((LANES, 1), 0).astype(jnp.int16)
-    high_row = iota((16, 1), 0).astype(jnp.int16)
-    count = jnp.zeros((LANES, 16), F32)
+    few = 32
+    row_index = iota((few, 1), 0).astype(jnp.int16)
+    count = jnp.zeros((few, few), F32)
     for ref in [lists_ref] + [send_ref.at[g] for g in range(groups)]:
         index = ref[...]
-        low = (index & (LANES - 1)).astype(jnp.int16)
-        high = (index >> 7).astype(jnp.int16)
+        low = (index & (few - 1)).astype(jnp.int16)
+        high = (index >> 5).astype(jnp.int16)
         for k in range(index.shape[0]):
-            count += dot(match(low[k : k + 1], low_row), match(high[k : k + 1], high_row), LAST)
-    node = jnp.sum(grad_agg, axis=0, keepdims=True)
-    for h in range(rows // LANES):
-        carried = wire[h * LANES : (h + 1) * LANES].astype(F32) * count[:, h : h + 1]
-        node += jnp.sum(carried, axis=0, keepdims=True)
+            count += dot(match(low[k : k + 1], row_index), match(high[k : k + 1], row_index), LAST)
+    carried = jnp.zeros((few, out.shape[1]), F32)
+    for h in range(rows // few):
+        carried += wire[h * few : (h + 1) * few].astype(F32) * count[:, h : h + 1]
+    node = jnp.sum(grad_agg, axis=0, keepdims=True) + jnp.sum(carried, axis=0, keepdims=True)
 
     part_w1 = dot(saved_ref[...], grad_z, FIRST)
     part_w2 = dot(out, hidden, FIRST)
@@ -138,10 +143,11 @@
     for step, (wide, thin) in enumerate(quarters):
         if step:
             choose(step)
-        rows_ref[step, rows : rows + LANES, :] = wide.astype(BF16)
-        rows_ref[step, rows + LANES :, :] = remainders(wide, columns(thin))
+        rows_ref[step, half:, :LANES] = wide.astype(BF16)
+        rows_ref[step, half:, LANES:] = remainders(wide, columns(thin))
         own = pl.ds(step * block, block)
-        piece_ref[own, :] = dot(chosen_ref[step], rows_ref[step]).astype(BF16)
+        both = dot(chosen_ref[step], rows_ref[step]).astype(BF16)
+        piece_ref[own, :] = jnp.where(index_ref[step] >= half, both[:, LANES:], both[:, :LANES])
         copy = pltpu.make_async_copy(piece_ref.at[own], piece_hbm.at[own], out_sems.at[2 + step])
         copy.start()
         departures.append(copy)
@@ -245,8 +251,9 @@
         + [pltpu.VMEM(*out) for out in outs]
         + [
             pltpu.SemaphoreType.DMA((2 + blocks,)),
-            pltpu.VMEM((blocks, rows + 2 * LANES, width), BF16),
-            pltpu.VMEM((blocks, LANES * piece, rows + 2 * LANES), BF16),
+            pltpu.VMEM((blocks, rows // 2 + LANES, 2 * width), BF16),
+            pltpu.VMEM((blocks, LANES * piece, rows // 2 + LANES), BF16),
+            pltpu.VMEM((blocks, LANES * piece, LANES), jnp.int16),
         ],
         far=len(sources),
         limit=60,

time: 95.6 us -> 93.8 us (0.981)
  Pallas kernels: 13.9 us -> 12.1 us
    pallas_call x1, Pallas kernels: 6.72 us -> 4.94 us  [per_device(): call(first_kernel, outs, [pltpu.VMEM(x.shape, x.dtype) for x in sources]...]
where the time goes in v4:
time: 93.8 us; the launch traced here: 93.6 us
  blocking collectives  59.9 us (64%)
  Pallas kernels  12.1 us (13%)
  waiting for transfers between devices  10.6 us (11%)
  starting transfers between devices  9.67 us (10%)
    all_to_all x1, blocking collectives, exchange(): lax.all_to_all(x, AXES, split_axis=0, concat_axis=0, tiled=True)  59.9 us
    all_to_all x1, waiting for transfers between devices, exchange(): lax.all_to_all(x, AXES, split_axis=0, concat_axis=0, tiled=True)  10.6 us
    all_to_all x1, starting transfers between devices, exchange(): lax.all_to_all(x, AXES, split_axis=0, concat_axis=0, tiled=True)  9.67 us
    pallas_call x1, Pallas kernels, per_device(): call(first_kernel, outs, [pltpu.VMEM(x.shape, x.dtype) for x in sources]...  4.94 us
    pallas_call x1, Pallas kernels, per_device(): call(remote_kernel, [((rows, width), BF16)], flops=2 * devices * piece *...  2.87 us
    pallas_call x1, Pallas kernels, per_device(): call(local_kernel, [((rows, width), F32), ((devices * piece // LANES, LAN...  2.4 us
  transfers between devices with their start and end apart: 1, of which 1 were waited for; matrix products, arithmetic and copies ran while one was open for 0% of the time, Pallas kernels for 6%

profile of v4, /device:TPU:1, one launch (start us, length us, event | category | flops | bytes accessed | tf_op | source)
XLA Modules:
  0.0 93.6 jit_solution(9727503548159110520)
XLA Ops:
  0.6 4.9 %shard_map.127 = (bf16[5120,128]{1,0:T(8,128)(2,1)}, f32[768,128]{1,0:T(8,128)}, bf16[768,128]{1,0:T(8,128)(2,1)}) custom-call(s32[4,8,128]{2,1,0:T(8,128)} %bitcast.21, bf16[768,128]{1,0:T(8,128)(2,1)} %out_hbm.1, bf16[256,128]{1,0:T(8,128)(2,1)} %w2_hbm.1, bf16[768,256]{1,0:T(8,128)(2,1)} %hid_hbm.1, bf16[128,256]{1,0:T(8,128)(2,1)} %w1_hbm.1, ...), custom_call_target="tpu_custom_call" | custom-call | flops 1006632960 | bytes 1310720 | tf_op jit(solution)/shard_map/pallas_call | solution.py:246
  5.6 59.9 %all_to_all.10 = bf16[512,5,2,128]{3,2,1,0:T(2,128)(2,1)S(1)} all-to-all(bf16[512,5,2,128]{3,2,1,0:T(2,128)(2,1)} %bitcast.19), channel_id=1, replica_groups=mesh['nodes'=128,'grp'=4] {'nodes','grp'}, dimensions={0} | all-to-all | bytes 2621440 | tf_op jit(solution)/shard_map/all_to_all | solution.py:274
  65.5 0.0 copy-start.3
  65.5 0.0 copy-start
  65.5 0.0 copy-start.1
  65.5 0.0 copy-start.2
  65.5 1.1 %shard_map.130 = bf16[1024,128]{1,0:T(8,128)(2,1)} custom-call(bf16[5120,128]{1,0:T(8,128)(2,1)S(1)} %bitcast.14), custom_call_target="tpu_custom_call" | custom-call | flops 20971520 | bytes 1310720 | tf_op jit(solution)/shard_map/pallas_call | solution.py:277
  66.6 9.7 %all-to-all-start.1 = ((bf16[512,1,2,128]{3,2,1,0:T(2,128)(2,1)}), bf16[512,1,2,128]{3,2,1,0:T(2,128)(2,1)S(1)}, u32[]{:S(2)}, u32[]{:S(2)}) async-start(bf16[512,1,2,128]{3,2,1,0:T(2,128)(2,1)} %bitcast.7), calls=%async_computation.1 | async-start | bytes 524288 | tf_op jit(solution)/shard_map/all_to_all | solution.py:274
  76.3 0.0 copy-done.3
  76.3 0.1 copy.18
  76.5 0.3 reshape.27.recv_ref
  76.8 0.0 copy-done
  76.8 0.0 copy-done.1
  76.8 0.0 copy-done.2
  76.8 2.4 %shard_map.128 = (f32[768,128]{1,0:T(8,128)S(1)}, s32[40,128]{1,0:T(8,128)S(1)}) custom-call(s32[16,768]{1,0:T(8,128)S(1)} %bitcast.18, s32[40,128]{1,0:T(8,128)S(1)} %reshape.27.recv_ref, bf16[768,128]{1,0:T(8,128)(2,1)S(1)} %copy-done.1, f32[768,128]{1,0:T(8,128)S(1)} %copy-done), custom_call_target="tpu_custom_call" | custom-call | flops 150994944 | bytes 983040 | tf_op jit(solution)/shard_map/pallas_call | solution.py:264
  79.2 2.9 %shard_map.129 = bf16[768,128]{1,0:T(8,128)(2,1)} custom-call(s32[40,128]{1,0:T(8,128)S(1)} %get-tuple-element.18.recv_ref, bf16[5120,128]{1,0:T(8,128)(2,1)S(1)} %bitcast.15, f32[768,128]{1,0:T(8,128)S(1)} %get-tuple-element.20.total_ref), custom_call_target="tpu_custom_call" | custom-call | flops 1006632960 | bytes 1310720 | tf_op jit(solution)/shard_map/pallas_call | solution.py:284
  82.1 10.6 %all-to-all-done.1 = bf16[512,1,2,128]{3,2,1,0:T(2,128)(2,1)S(1)} async-done(((bf16[512,1,2,128]{3,2,1,0:T(2,128)(2,1)}), bf16[512,1,2,128]{3,2,1,0:T(2,128)(2,1)S(1)}, u32[]{:S(2)}, u32[]{:S(2)}) %all-to-all-start.1) | async-done | bytes 262176 | tf_op jit(solution)/shard_map/all_to_all | solution.py:274
  92.7 0.8 shard_map.131
  (1 shorter events, 0.0 us)
Async XLA Ops:
  65.5 10.8 %copy-start.3 = (s32[1,1,128,4,8]{2,4,3,1,0:T(8,128)S(1)}, s32[1,1,128,4,8]{2,4,3,1,0:T(8,128)}, u32[]{:S(2)}) copy-start(s32[1,1,128,4,8]{2,4,3,1,0:T(8,128)} %param.15) | copy-start | bytes 49156
  65.5 11.3 %copy-start = (f32[768,128]{1,0:T(8,128)S(1)}, f32[768,128]{1,0:T(8,128)}, u32[]{:S(2)}) copy-start(f32[768,128]{1,0:T(8,128)} %get-tuple-element.17.agg_ref) | copy-start | bytes 1179652
  65.5 11.3 %copy-start.1 = (bf16[768,128]{1,0:T(8,128)(2,1)S(1)}, bf16[768,128]{1,0:T(8,128)(2,1)}, u32[]{:S(2)}) copy-start(bf16[768,128]{1,0:T(8,128)(2,1)} %get-tuple-element.16.wire_ref) | copy-start | bytes 589828
  65.5 11.3 %copy-start.2 = (s32[768,16]{0,1:T(8,128)S(1)}, s32[768,16]{0,1:T(8,128)}, u32[]{:S(2)}) copy-start(s32[768,16]{0,1:T(8,128)} %param.13) | copy-start | bytes 147460
  66.6 26.1 %all-to-all-start.1 = ((bf16[512,1,2,128]{3,2,1,0:T(2,128)(2,1)}), bf16[512,1,2,128]{3,2,1,0:T(2,128)(2,1)S(1)}, u32[]{:S(2)}, u32[]{:S(2)}) async-start(bf16[512,1,2,128]{3,2,1,0:T(2,128)(2,1)} %bitcast.7), calls=%async_computation.1 | async-start | bytes 524288 | tf_op jit(solution)/shard_map/all_to_all | solution.py:274

commit v5 on v4

--- a/solution.py
+++ b/solution.py
@@ -44,57 +44,43 @@
     return jnp.where(lane == LANES - 1, low_part(thin), low).astype(BF16)
 
 
-def first_kernel(
-    send_hbm, out_hbm, w2_hbm, hid_hbm, w1_hbm, lists_hbm, saved_hbm,
-    piece_hbm, agg_hbm, wire_hbm,
-    send_ref, out_ref, w2_ref, hid_ref, w1_ref, lists_ref, saved_ref, in_sems,
-    piece_ref, agg_ref, wire_ref, out_sems,
-    rows_ref, chosen_ref, index_ref,
-):
+def choose(half, steps, send_ref, chosen_ref, index_ref):
     groups, slots, nodes = send_ref.shape
-    rows = out_ref.shape[0]
+    block = chosen_ref.shape[1]
     piece = slots + EXTRA
-    block = LANES * piece
     width = LANES // groups
-    blocks = nodes // width
-    pairs = [
-        (send_hbm, send_ref), (out_hbm, out_ref), (w2_hbm, w2_ref), (hid_hbm, hid_ref),
-        (w1_hbm, w1_ref), (lists_hbm, lists_ref), (saved_hbm, saved_ref),
-    ]
-    arrivals = [pltpu.make_async_copy(a, b, in_sems.at[i]) for i, (a, b) in enumerate(pairs)]
-    for copy in arrivals:
-        copy.start()
-
-    half = rows // 2
     place = jnp.where(
         iota((block, LANES), 0) // piece * piece == piece * iota((block, LANES), 1), 1.0, 0.0
     )
     place = jnp.where(iota((block, LANES), 0) % piece >= slots, place, 0.0).astype(BF16)
-    for step in range(blocks):
-        chosen_ref[step, :, half:] = place
-
-    arrivals[0].wait()
     parts = []
     for g in range(groups):
-        parts += [send_ref[g], jnp.full((1, nodes), -1, jnp.int32), jnp.full((1, nodes), 2 * rows, jnp.int32)]
+        parts += [send_ref[g], jnp.full((1, nodes), -1, jnp.int32), jnp.full((1, nodes), 4 * half, jnp.int32)]
     sent = jnp.concatenate(parts, axis=0)
     sent = jnp.concatenate([sent, pltpu.roll(sent, nodes - 1, 1)], axis=0).astype(jnp.int16)
     lane_index = iota((16, half), 1).astype(jnp.int16)
-
-    def choose(step):
+    for i, step in enumerate(steps):
+        chosen_ref[i, :, half:] = place
         for n in range(0, width, 2):
             for r in range(0, 2 * groups * piece, 16):
                 at = step * width + n
                 start = n * groups * piece + r
                 index = jnp.broadcast_to(sent[r : r + 16, at : at + 1], (16, LANES))
-                index_ref[step, start : start + 16, :] = index
+                index_ref[i, start : start + 16, :] = index
                 folded = jnp.where(index >= half, index - half, index)
                 for t in range(0, half, LANES):
-                    chosen_ref[step, start : start + 16, t : t + LANES] = match(folded, lane_index[:, t : t + LANES])
-
-    choose(0)
-    for copy in arrivals[1:5]:
-        copy.wait()
+                    chosen_ref[i, start : start + 16, t : t + LANES] = match(folded, lane_index[:, t : t + LANES])
+
+
+def first_kernel(
+    chosen_ref, index_ref, send_ref, out_ref, w2_ref, hid_ref, w1_ref, lists_ref, saved_ref,
+    piece_ref, agg_ref, wire_ref, rows_ref, more_chosen_ref, more_index_ref,
+):
+    early, block, _ = chosen_ref.shape
+    blocks = rows_ref.shape[0]
+    groups = send_ref.shape[0]
+    rows = out_ref.shape[0]
+    half = rows // 2
     out = out_ref[...]
     hidden = hid_ref[...]
     grad_hidden = dot(out, w2_ref[...], LAST)
@@ -103,17 +89,10 @@
     wire = grad_agg.astype(BF16)
     agg_ref[...] = grad_agg
     wire_ref[...] = wire
-    departures = [
-        pltpu.make_async_copy(agg_ref, agg_hbm, out_sems.at[0]),
-        pltpu.make_async_copy(wire_ref, wire_hbm, out_sems.at[1]),
-    ]
-    for copy in departures:
-        copy.start()
     for step in range(blocks):
         rows_ref[step, :half, :LANES] = wire[:half]
         rows_ref[step, :half, LANES:] = wire[half:]
-    for copy in arrivals[5:]:
-        copy.wait()
+    choose(half, range(early, blocks), send_ref, more_chosen_ref, more_index_ref)
 
     few = 32
     row_index = iota((few, 1), 0).astype(jnp.int16)
@@ -141,18 +120,14 @@
     ]
 
     for step, (wide, thin) in enumerate(quarters):
-        if step:
-            choose(step)
         rows_ref[step, half:, :LANES] = wide.astype(BF16)
         rows_ref[step, half:, LANES:] = remainders(wide, columns(thin))
-        own = pl.ds(step * block, block)
-        both = dot(chosen_ref[step], rows_ref[step]).astype(BF16)
-        piece_ref[own, :] = jnp.where(index_ref[step] >= half, both[:, LANES:], both[:, :LANES])
-        copy = pltpu.make_async_copy(piece_ref.at[own], piece_hbm.at[own], out_sems.at[2 + step])
-        copy.start()
-        departures.append(copy)
-    for copy in departures:
-        copy.wait()
+        selects, indices = (chosen_ref, index_ref) if step < early else (more_chosen_ref, more_index_ref)
+        at = step if step < early else step - early
+        both = dot(selects[at], rows_ref[step]).astype(BF16)
+        piece_ref[step * block : (step + 1) * block, :] = jnp.where(
+            indices[at] >= half, both[:, LANES:], both[:, :LANES]
+        )
 
 
 def local_kernel(lists_ref, recv_ref, wire_ref, agg_ref, total_ref, target_ref, counts_ref):
@@ -217,16 +192,13 @@
     node_ref[...] = thin[3]
 
 
-def call(kernel, outs, scratch=(), far=0, limit=24, **cost):
-    hbm = pl.BlockSpec(memory_space=pltpu.HBM)
-    specs = {"in_specs": [hbm] * far, "out_specs": [hbm] * len(outs)} if far else {}
+def call(kernel, outs, scratch=(), limit=24, **cost):
     return pl.pallas_call(
         kernel,
         out_shape=[jax.ShapeDtypeStruct(shape, dtype) for shape, dtype in outs],
         scratch_shapes=list(scratch),
         compiler_params=pltpu.CompilerParams(vmem_limit_bytes=limit << 20),
         cost_estimate=pl.CostEstimate(transcendentals=0, **cost),
-        **specs,
     )
 
 
@@ -240,26 +212,29 @@
     piece = slots + EXTRA
     lists = local_lists.T
     send = jnp.transpose(send_slots[0, 0], (1, 2, 0))
-    sources = [send, grad_out, w_two, hidden_saved, w_one, lists, agg_saved]
-    outs = [((devices * piece, width), BF16), ((rows, width), F32), ((rows, width), BF16)]
     blocks = devices // LANES
+    depth = rows // 2 + LANES
+    early = blocks // 2
+
+    def shapes(n):
+        return [((n, LANES * piece, depth), BF16), ((n, LANES * piece, LANES), jnp.int16)]
+
+    chosen, index = call(
+        functools.partial(choose, rows // 2, range(early)),
+        shapes(early),
+        flops=2 * 10**9,
+        bytes_accessed=early * LANES * piece * depth * 2,
+        limit=8,
+    )(send)
     pieces, agg, wire = call(
         first_kernel,
-        outs,
-        [pltpu.VMEM(x.shape, x.dtype) for x in sources]
-        + [pltpu.SemaphoreType.DMA((len(sources),))]
-        + [pltpu.VMEM(*out) for out in outs]
-        + [
-            pltpu.SemaphoreType.DMA((2 + blocks,)),
-            pltpu.VMEM((blocks, rows // 2 + LANES, 2 * width), BF16),
-            pltpu.VMEM((blocks, LANES * piece, rows // 2 + LANES), BF16),
-            pltpu.VMEM((blocks, LANES * piece, LANES), jnp.int16),
-        ],
-        far=len(sources),
-        limit=60,
-        flops=2 * devices * piece * rows * width,
-        bytes_accessed=devices * piece * width * 2,
-    )(*sources)
+        [((devices * piece, width), BF16), ((rows, width), F32), ((rows, width), BF16)],
+        [pltpu.VMEM((blocks, depth, 2 * width), BF16)]
+        + [pltpu.VMEM(*shape) for shape in shapes(blocks - early)],
+        limit=16,
+        flops=4 * devices * piece * depth * width,
+        bytes_accessed=devices * piece * depth * 2,
+    )(chosen, index, send, grad_out, w_two, hidden_saved, w_one, lists, agg_saved)
     recv = jnp.pad(receive_slots[0, 0], ((0, 0), (0, 0), (0, EXTRA)), constant_values=rows)
     total, targets = call(
         local_kernel,

time: 93.8 us -> 93.2 us (level)
  Pallas kernels: 12.1 us -> 10.8 us
    pallas_call x1 -> x2, Pallas kernels: 4.94 us -> 3.61 us  [the longest x1 2.64 us: per_device(): call(first_kernel, [((devices * piece, width), BF16), ((rows, width), F32...]
  transfers between devices with their start and end apart: 1 -> 1, of which waited for: 1 -> 1; matrix products, arithmetic and copies ran while one was open for 0% -> 1% of each run, Pallas kernels for 6% -> 6%
where the time goes in v5:
time: 93.2 us; the launch traced here: 93 us
  blocking collectives  59.7 us (64%)
  Pallas kernels  10.8 us (12%)
  waiting for transfers between devices  10.7 us (11%)
  starting transfers between devices  9.67 us (10%)
  local copies, waits for them, and re-layouts  1.33 us (1%)
    all_to_all x1, blocking collectives, exchange(): lax.all_to_all(x, AXES, split_axis=0, concat_axis=0, tiled=True)  59.7 us
    all_to_all x1, waiting for transfers between devices, exchange(): lax.all_to_all(x, AXES, split_axis=0, concat_axis=0, tiled=True)  10.7 us
    all_to_all x1, starting transfers between devices, exchange(): lax.all_to_all(x, AXES, split_axis=0, concat_axis=0, tiled=True)  9.67 us
    pallas_call x1, Pallas kernels, per_device(): call(remote_kernel, [((rows, width), BF16)], flops=2 * devices * piece *...  2.87 us
    pallas_call x1, Pallas kernels, per_device(): call(first_kernel, [((devices * piece, width), BF16), ((rows, width), F32...  2.64 us
    pallas_call x1, Pallas kernels, per_device(): call(local_kernel, [((rows, width), F32), ((devices * piece // LANES, LAN...  2.4 us
  transfers between devices with their start and end apart: 1, of which 1 were waited for; matrix products, arithmetic and copies ran while one was open for 1% of the time, Pallas kernels for 6%

profile of v5, /device:TPU:1, one launch (start us, length us, event | category | flops | bytes accessed | tf_op | source)
XLA Modules:
  0.0 93.0 jit_solution(17484745865906179195)
XLA Ops:
  0.6 0.0 copy-start.6
  0.6 0.7 copy-done.6
  1.4 0.0 copy-start
  1.4 0.0 copy-start.1
  1.4 0.0 copy-start.2
  1.4 0.0 copy-start.3
  1.4 0.0 copy-start.4
  1.4 0.0 copy-start.5
  1.4 0.0 copy-start.7
  1.4 1.0 %shard_map.127 = (bf16[2,1280,512]{2,1,0:T(8,128)(2,1)S(1)}, s16[2,1280,128]{2,1,0:T(8,128)(2,1)S(1)}) custom-call(s32[4,8,128]{2,1,0:T(8,128)S(1)} %bitcast.20), custom_call_target="tpu_custom_call" | custom-call | flops 2000000000 | bytes 2621440 | tf_op jit(solution)/shard_map/pallas_call | solution.py:222
  2.4 0.0 copy-done
  2.4 0.0 copy-done.1
  2.4 0.0 copy-done.2
  2.4 0.1 copy-done.3
  2.5 0.0 copy-done.4
  2.5 0.0 copy-done.5
  2.5 0.0 copy-done.7
  2.5 2.6 %shard_map.128 = (bf16[5120,128]{1,0:T(8,128)(2,1)S(1)}, f32[768,128]{1,0:T(8,128)S(1)}, bf16[768,128]{1,0:T(8,128)(2,1)S(1)}) custom-call(bf16[2,1280,512]{2,1,0:T(8,128)(2,1)S(1)} %get-tuple-element.18.chosen_ref, s16[2,1280,128]{2,1,0:T(8,128)(2,1)S(1)} %get-tuple-element.19.index_ref, s32[4,8,128]{2,1,0:T(8,128)S(1)} %bitcast.21, ...), custom_call_target="tpu_custom_call" | custom-call | flops 1342177280 | bytes 5242880 | tf_op jit(solution)/shard_map/pallas_call | solution.py:229
  5.2 59.7 %all_to_all.10 = bf16[512,5,2,128]{3,2,1,0:T(2,128)(2,1)S(1)} all-to-all(bf16[512,5,2,128]{3,2,1,0:T(2,128)(2,1)S(1)} %bitcast.16), channel_id=1, replica_groups=mesh['nodes'=128,'grp'=4] {'nodes','grp'}, dimensions={0} | all-to-all | bytes 2621440 | tf_op jit(solution)/shard_map/all_to_all | solution.py:249
  64.9 0.0 copy-start.8
  64.9 1.1 %shard_map.131 = bf16[1024,128]{1,0:T(8,128)(2,1)} custom-call(bf16[5120,128]{1,0:T(8,128)(2,1)S(1)} %bitcast.14), custom_call_target="tpu_custom_call" | custom-call | flops 20971520 | bytes 1310720 | tf_op jit(solution)/shard_map/pallas_call | solution.py:252
  66.0 9.7 %all-to-all-start.1 = ((bf16[512,1,2,128]{3,2,1,0:T(2,128)(2,1)}), bf16[512,1,2,128]{3,2,1,0:T(2,128)(2,1)S(1)}, u32[]{:S(2)}, u32[]{:S(2)}) async-start(bf16[512,1,2,128]{3,2,1,0:T(2,128)(2,1)} %bitcast.7), calls=%async_computation.1 | async-start | bytes 524288 | tf_op jit(solution)/shard_map/all_to_all | solution.py:249
  75.7 0.0 copy-done.8
  75.7 0.1 copy.18
  75.9 0.3 reshape.27.recv_ref
  76.2 2.4 %shard_map.129 = (f32[768,128]{1,0:T(8,128)S(1)}, s32[40,128]{1,0:T(8,128)S(1)}) custom-call(s32[16,768]{1,0:T(8,128)S(1)} %bitcast.19, s32[40,128]{1,0:T(8,128)S(1)} %reshape.27.recv_ref, bf16[768,128]{1,0:T(8,128)(2,1)S(1)} %get-tuple-element.20.wire_ref, f32[768,128]{1,0:T(8,128)S(1)} %get-tuple-element.21.agg_ref), custom_call_target="tpu_custom_call" | custom-call | flops 150994944 | bytes 983040 | tf_op jit(solution)/shard_map/pallas_call | solution.py:239
  78.6 2.9 %shard_map.130 = bf16[768,128]{1,0:T(8,128)(2,1)} custom-call(s32[40,128]{1,0:T(8,128)S(1)} %get-tuple-element.22.recv_ref, bf16[5120,128]{1,0:T(8,128)(2,1)S(1)} %bitcast.15, f32[768,128]{1,0:T(8,128)S(1)} %get-tuple-element.24.total_ref), custom_call_target="tpu_custom_call" | custom-call | flops 1006632960 | bytes 1310720 | tf_op jit(solution)/shard_map/pallas_call | solution.py:259
  81.4 10.7 %all-to-all-done.1 = bf16[512,1,2,128]{3,2,1,0:T(2,128)(2,1)S(1)} async-done(((bf16[512,1,2,128]{3,2,1,0:T(2,128)(2,1)}), bf16[512,1,2,128]{3,2,1,0:T(2,128)(2,1)S(1)}, u32[]{:S(2)}, u32[]{:S(2)}) %all-to-all-start.1) | async-done | bytes 262176 | tf_op jit(solution)/shard_map/all_to_all | solution.py:249
  92.1 0.8 shard_map.132
  (1 shorter events, 0.0 us)
Async XLA Ops:
  0.6 0.7 copy-start.6
  1.4 1.0 %copy-start = (s32[768,16]{0,1:T(8,128)S(1)}, s32[768,16]{0,1:T(8,128)}, u32[]{:S(2)}) copy-start(s32[768,16]{0,1:T(8,128)} %param.13) | copy-start | bytes 147460
  1.4 1.0 %copy-start.1 = (bf16[768,256]{1,0:T(8,128)(2,1)S(1)}, bf16[768,256]{1,0:T(8,128)(2,1)}, u32[]{:S(2)}) copy-start(bf16[768,256]{1,0:T(8,128)(2,1)} %hid_ref.1) | copy-start | bytes 1179652
  1.4 1.1 %copy-start.2 = (bf16[768,128]{1,0:T(8,128)(2,1)S(1)}, bf16[768,128]{1,0:T(8,128)(2,1)}, u32[]{:S(2)}) copy-start(bf16[768,128]{1,0:T(8,128)(2,1)} %out_ref.1) | copy-start | bytes 589828
  1.4 1.2 %copy-start.3 = (bf16[768,128]{1,0:T(8,128)(2,1)S(1)}, bf16[768,128]{1,0:T(8,128)(2,1)}, u32[]{:S(2)}) copy-start(bf16[768,128]{1,0:T(8,128)(2,1)} %saved_ref.1) | copy-start | bytes 589828
  1.4 1.2 %copy-start.4 = (bf16[256,128]{1,0:T(8,128)(2,1)S(1)}, bf16[256,128]{1,0:T(8,128)(2,1)}, u32[]{:S(2)}) copy-start(bf16[256,128]{1,0:T(8,128)(2,1)} %w2_ref.1) | copy-start | bytes 196612
  1.4 1.2 %copy-start.5 = (bf16[128,256]{1,0:T(8,128)(2,1)S(1)}, bf16[128,256]{1,0:T(8,128)(2,1)}, u32[]{:S(2)}) copy-start(bf16[128,256]{1,0:T(8,128)(2,1)} %w1_ref.1) | copy-start | bytes 196612
  1.4 1.1 %copy-start.7 = (s32[1,1,128,4,8]{2,4,3,1,0:T(8,128)S(1)}, s32[1,1,128,4,8]{2,4,3,1,0:T(8,128)}, u32[]{:S(2)}) copy-start(s32[1,1,128,4,8]{2,4,3,1,0:T(8,128)} %param.14) | copy-start | bytes 49156
  64.9 10.8 %copy-start.8 = (s32[1,1,128,4,8]{2,4,3,1,0:T(8,128)S(1)}, s32[1,1,128,4,8]{2,4,3,1,0:T(8,128)}, u32[]{:S(2)}) copy-start(s32[1,1,128,4,8]{2,4,3,1,0:T(8,128)} %param.15) | copy-start | bytes 49156
  66.0 26.1 %all-to-all-start.1 = ((bf16[512,1,2,128]{3,2,1,0:T(2,128)(2,1)}), bf16[512,1,2,128]{3,2,1,0:T(2,128)(2,1)S(1)}, u32[]{:S(2)}, u32[]{:S(2)}) async-start(bf16[512,1,2,128]{3,2,1,0:T(2,128)(2,1)} %bitcast.7), calls=%async_computation.1 | async-start | bytes 524288 | tf_op jit(solution)/shard_map/all_to_all | solution.py:249

commit v6 on v5

--- a/solution.py
+++ b/solution.py
@@ -5,6 +5,7 @@
 from jax import lax
 from jax.experimental import pallas as pl
 from jax.experimental.pallas import tpu as pltpu
+from jax.sharding import Mesh
 from jax.sharding import PartitionSpec as P
 
 BF16 = jnp.bfloat16
@@ -14,7 +15,8 @@
 FIRST = (((0,), (0,)), ((), ()))
 LANES = 128
 EXTRA = 2
-AXES = ("nodes", "grp")
+CORES = 2
+AXES = ("chips", "core", "grp")
 
 
 def dot(a, b, dims=PLAIN):
@@ -49,10 +51,11 @@
     block = chosen_ref.shape[1]
     piece = slots + EXTRA
     width = LANES // groups
-    place = jnp.where(
-        iota((block, LANES), 0) // piece * piece == piece * iota((block, LANES), 1), 1.0, 0.0
-    )
-    place = jnp.where(iota((block, LANES), 0) % piece >= slots, place, 0.0).astype(BF16)
+    row, lane = iota((block, LANES), 0), iota((block, LANES), 1)
+    share = LANES // CORES
+    owner = (lane % share // groups * CORES + lane // share) * groups + lane % groups
+    place = jnp.where(row // piece == owner, 1.0, 0.0)
+    place = jnp.where(row % piece >= slots, place, 0.0).astype(BF16)
     parts = []
     for g in range(groups):
         parts += [send_ref[g], jnp.full((1, nodes), -1, jnp.int32), jnp.full((1, nodes), 4 * half, jnp.int32)]
@@ -119,9 +122,15 @@
         (part_w2[:, LANES:], node),
     ]
 
-    for step, (wide, thin) in enumerate(quarters):
-        rows_ref[step, half:, :LANES] = wide.astype(BF16)
-        rows_ref[step, half:, LANES:] = remainders(wide, columns(thin))
+    share = LANES // CORES
+    for q, (wide, thin) in enumerate(quarters):
+        high, low = wide.astype(BF16), remainders(wide, columns(thin))
+        core, first = q // 2, q % 2 * CORES
+        for c in range(CORES):
+            to = slice(half + core * share, half + (core + 1) * share)
+            rows_ref[first + c, to, :LANES] = high[c * share : (c + 1) * share]
+            rows_ref[first + c, to, LANES:] = low[c * share : (c + 1) * share]
+    for step in range(blocks):
         selects, indices = (chosen_ref, index_ref) if step < early else (more_chosen_ref, more_index_ref)
         at = step if step < early else step - early
         both = dot(selects[at], rows_ref[step]).astype(BF16)
@@ -172,11 +181,14 @@
     x_ref[...] = total.astype(BF16)
 
 
-def last_kernel(share_ref, w1_ref, b1_ref, w2_ref, b2_ref, node_ref, rows_ref):
-    rows_ref[...] = share_ref[...].astype(F32)
-    half = rows_ref.shape[0] // 2
-    high = rows_ref[pl.ds(0, half, 2), :]
-    low = rows_ref[pl.ds(1, half, 2), :]
+def last_kernel(core_ref, mine_ref, mate_ref, w1_ref, b1_ref, w2_ref, b2_ref, node_ref, rows_ref):
+    first = core_ref[0] == 0
+    count = mine_ref.shape[0]
+    mine, mate = mine_ref[...].astype(F32), mate_ref[...].astype(F32)
+    rows_ref[:count, :] = jnp.where(first, mine, mate)
+    rows_ref[count : 2 * count, :] = jnp.where(first, mate, mine)
+    high = rows_ref[pl.ds(0, count, 2), :]
+    low = rows_ref[pl.ds(1, count, 2), :]
     lane = iota(high.shape, 1)
     wide = high + jnp.where(lane >= LANES - 2, 0.0, low)
     w1_ref[:, :LANES] = wide[:LANES]
@@ -192,13 +204,15 @@
     node_ref[...] = thin[3]
 
 
-def call(kernel, outs, scratch=(), limit=24, **cost):
+def call(kernel, outs, scratch=(), limit=24, specs=None, **cost):
+    extra = {"in_specs": specs} if specs else {}
     return pl.pallas_call(
         kernel,
         out_shape=[jax.ShapeDtypeStruct(shape, dtype) for shape, dtype in outs],
         scratch_shapes=list(scratch),
         compiler_params=pltpu.CompilerParams(vmem_limit_bytes=limit << 20),
         cost_estimate=pl.CostEstimate(transcendentals=0, **cost),
+        **extra,
     )
 
 
@@ -244,24 +258,26 @@
         bytes_accessed=rows * width * 10,
     )(lists, recv.reshape(-1, LANES), wire, agg)
 
-    def exchange(x, height):
-        x = x.reshape(devices, height // 2, 2, width)
-        return lax.all_to_all(x, AXES, split_axis=0, concat_axis=0, tiled=True).reshape(-1, width)
-
-    arrived = exchange(pieces, piece)
+    def exchange(x, height, axes):
+        x = x.reshape(-1, height // 2, 2, width)
+        return lax.all_to_all(x, axes, split_axis=0, concat_axis=0, tiled=True).reshape(-1, width)
+
+    arrived = exchange(pieces, piece, AXES)
     (share,) = call(
         functools.partial(chunk_kernel, piece, 1.0 / devices),
-        [((devices * EXTRA, width), BF16)],
+        [((devices // CORES * EXTRA, width), BF16)],
         flops=2 * 16 * devices * piece * width,
         bytes_accessed=devices * piece * width * 2,
     )(arrived)
-    shares = exchange(share, EXTRA)
+    mine = exchange(share, EXTRA, ("chips", "grp"))
     (grad_x,) = call(
         remote_kernel,
         [((rows, width), BF16)],
         flops=2 * devices * piece * rows * width,
         bytes_accessed=devices * piece * width * 2,
     )(targets, arrived, total)
+    grad_x, mine = lax.optimization_barrier((grad_x, mine))
+    mate = lax.ppermute(mine, "core", [(c, CORES - 1 - c) for c in range(CORES)])
     w1, b1, w2, b2, node = call(
         last_kernel,
         [
@@ -271,14 +287,17 @@
             ((1, width), F32),
             ((1, width), F32),
         ],
-        [pltpu.VMEM((devices * EXTRA, width), F32)],
+        [pltpu.VMEM((devices * EXTRA + 8, width), F32)],
+        specs=[pl.BlockSpec(memory_space=pltpu.SMEM)] + [pl.BlockSpec(memory_space=pltpu.VMEM)] * 2,
         flops=0,
         bytes_accessed=devices * EXTRA * width * 2,
-    )(shares)
+    )(lax.axis_index("core").astype(jnp.int32).reshape(1), mine, mate)
     return grad_x, w1, b1[0], w2, b2[0], node[0]
 
 
 def solution(mesh):
+    nodes, groups = mesh.devices.shape
+    chips = Mesh(mesh.devices.reshape(nodes // CORES, CORES, groups), AXES)
     placed = (
         P(AXES, None),
         P(AXES, None),
@@ -286,12 +305,12 @@
         P(),
         P(),
         P(AXES, None),
-        P("nodes", "grp", None, None, None),
-        P("nodes", "grp", None, None, None),
+        P(AXES[:2], "grp", None, None, None),
+        P(AXES[:2], "grp", None, None, None),
     )
     return jax.shard_map(
         per_device,
-        mesh=mesh,
+        mesh=chips,
         in_specs=placed,
         out_specs=(P(AXES, None), P(), P(), P(), P(), P()),
         check_vma=False,

time: 93.2 us -> 94.7 us (1.016)
  starting transfers between devices: 9.67 us -> 15 us
  waiting for transfers between devices: 10.7 us -> 6.9 us
    all_to_all x1, waiting for transfers between devices: 10.7 us -> 5.94 us  [exchange(): lax.all_to_all(x, axes, split_axis=0, concat_axis=0, tiled=True)]
    ppermute x0 -> x1, starting transfers between devices: none -> 4 us  [per_device(): lax.ppermute(mine, 'core', [(c, CORES - 1 - c) for c in range(CORES)])]
    all_to_all x1, starting transfers between devices: 9.67 us -> 11 us  [exchange(): lax.all_to_all(x, axes, split_axis=0, concat_axis=0, tiled=True)]
    ppermute x0 -> x1, waiting for transfers between devices: none -> 0.96 us  [per_device(): lax.ppermute(mine, 'core', [(c, CORES - 1 - c) for c in range(CORES)])]
  transfers between devices with their start and end apart: 1 -> 2, of which waited for: 1 -> 2; matrix products, arithmetic and copies ran while one was open for 1% -> 0% of each run, Pallas kernels for 6% -> 6%
where the time goes in v6:
time: 94.7 us; the launch traced here: 94.4 us
  blocking collectives  59.7 us (63%)
  starting transfers between devices  15 us (16%)
  Pallas kernels  10.8 us (11%)
  waiting for transfers between devices  6.9 us (7%)
  local copies, waits for them, and re-layouts  1.32 us (1%)
    all_to_all x1, blocking collectives, exchange(): lax.all_to_all(x, axes, split_axis=0, concat_axis=0, tiled=True)  59.7 us
    all_to_all x1, starting transfers between devices, exchange(): lax.all_to_all(x, axes, split_axis=0, concat_axis=0, tiled=True)  11 us
    all_to_all x1, waiting for transfers between devices, exchange(): lax.all_to_all(x, axes, split_axis=0, concat_axis=0, tiled=True)  5.94 us
    ppermute x1, starting transfers between devices, per_device(): lax.ppermute(mine, 'core', [(c, CORES - 1 - c) for c in range(CORES)])  4 us
    pallas_call x1, Pallas kernels, per_device(): call(remote_kernel, [((rows, width), BF16)], flops=2 * devices * piece *...  2.87 us
    pallas_call x1, Pallas kernels, per_device(): call(first_kernel, [((devices * piece, width), BF16), ((rows, width), F32...  2.64 us
    pallas_call x1, Pallas kernels, per_device(): call(local_kernel, [((rows, width), F32), ((devices * piece // LANES, LAN...  2.4 us
  transfers between devices with their start and end apart: 2, of which 2 were waited for; matrix products, arithmetic and copies ran while one was open for 0% of the time, Pallas kernels for 6%

profile of v6, /device:TPU:1, one launch (start us, length us, event | category | flops | bytes accessed | tf_op | source)
XLA Modules:
  0.0 94.4 jit_solution(5953510713060849167)
XLA Ops:
  0.6 0.0 copy-start.6
  0.6 0.7 copy-done.6
  1.4 0.0 copy-start
  1.4 0.0 copy-start.1
  1.4 0.0 copy-start.2
  1.4 0.0 copy-start.3
  1.4 0.0 copy-start.4
  1.4 0.0 copy-start.5
  1.4 0.0 copy-start.7
  1.4 1.0 %shard_map.127 = (bf16[2,1280,512]{2,1,0:T(8,128)(2,1)S(1)}, s16[2,1280,128]{2,1,0:T(8,128)(2,1)S(1)}) custom-call(s32[4,8,128]{2,1,0:T(8,128)S(1)} %bitcast.22), custom_call_target="tpu_custom_call" | custom-call | flops 2000000000 | bytes 2621440 | tf_op jit(solution)/shard_map/pallas_call | solution.py:236
  2.4 0.0 copy-done
  2.4 0.0 copy-done.1
  2.4 0.0 copy-done.2
  2.4 0.1 copy-done.3
  2.5 0.0 copy-done.4
  2.5 0.0 copy-done.5
  2.5 0.0 copy-done.7
  2.5 2.6 %shard_map.128 = (bf16[5120,128]{1,0:T(8,128)(2,1)S(1)}, f32[768,128]{1,0:T(8,128)S(1)}, bf16[768,128]{1,0:T(8,128)(2,1)S(1)}) custom-call(bf16[2,1280,512]{2,1,0:T(8,128)(2,1)S(1)} %get-tuple-element.20.chosen_ref, s16[2,1280,128]{2,1,0:T(8,128)(2,1)S(1)} %get-tuple-element.21.index_ref, s32[4,8,128]{2,1,0:T(8,128)S(1)} %bitcast.23, ...), custom_call_target="tpu_custom_call" | custom-call | flops 1342177280 | bytes 5242880 | tf_op jit(solution)/shard_map/pallas_call | solution.py:243
  5.2 59.7 %all_to_all.10 = bf16[512,5,2,128]{3,2,1,0:T(2,128)(2,1)S(1)} all-to-all(bf16[512,5,2,128]{3,2,1,0:T(2,128)(2,1)S(1)} %bitcast.17), channel_id=1, replica_groups=mesh['chips'=64,'core'=2,'grp'=4] {'chips','core','grp'}, dimensions={0} | all-to-all | bytes 2621440 | tf_op jit(solution)/shard_map/all_to_all | solution.py:263
  64.9 0.0 copy-start.8
  64.9 1.0 %shard_map.131 = bf16[512,128]{1,0:T(8,128)(2,1)} custom-call(bf16[5120,128]{1,0:T(8,128)(2,1)S(1)} %bitcast.15), custom_call_target="tpu_custom_call" | custom-call | flops 20971520 | bytes 1310720 | tf_op jit(solution)/shard_map/pallas_call | solution.py:266
  65.9 11.0 %all-to-all-start.1 = ((bf16[256,1,2,128]{3,2,1,0:T(2,128)(2,1)}), bf16[256,1,2,128]{3,2,1,0:T(2,128)(2,1)S(1)}, u32[]{:S(2)}, u32[]{:S(2)}) async-start(bf16[256,1,2,128]{3,2,1,0:T(2,128)(2,1)} %bitcast.7), calls=%async_computation.1 | async-start | bytes 262144 | tf_op jit(solution)/shard_map/all_to_all | solution.py:263
  76.9 0.0 copy-done.8
  76.9 0.1 copy.18
  77.1 0.3 reshape.30.recv_ref
  77.4 2.4 %shard_map.129 = (f32[768,128]{1,0:T(8,128)S(1)}, s32[40,128]{1,0:T(8,128)S(1)}) custom-call(s32[16,768]{1,0:T(8,128)S(1)} %bitcast.21, s32[40,128]{1,0:T(8,128)S(1)} %reshape.30.recv_ref, bf16[768,128]{1,0:T(8,128)(2,1)S(1)} %get-tuple-element.22.wire_ref, f32[768,128]{1,0:T(8,128)S(1)} %get-tuple-element.23.agg_ref), custom_call_target="tpu_custom_call" | custom-call | flops 150994944 | bytes 983040 | tf_op jit(solution)/shard_map/pallas_call | solution.py:253
  79.8 2.9 %shard_map.130 = bf16[768,128]{1,0:T(8,128)(2,1)} custom-call(s32[40,128]{1,0:T(8,128)S(1)} %get-tuple-element.24.recv_ref, bf16[5120,128]{1,0:T(8,128)(2,1)S(1)} %bitcast.16, f32[768,128]{1,0:T(8,128)S(1)} %get-tuple-element.26.total_ref), custom_call_target="tpu_custom_call" | custom-call | flops 1006632960 | bytes 1310720 | tf_op jit(solution)/shard_map/pallas_call | solution.py:273
  82.7 5.9 %all-to-all-done.1 = bf16[256,1,2,128]{3,2,1,0:T(2,128)(2,1)S(1)} async-done(((bf16[256,1,2,128]{3,2,1,0:T(2,128)(2,1)}), bf16[256,1,2,128]{3,2,1,0:T(2,128)(2,1)S(1)}, u32[]{:S(2)}, u32[]{:S(2)}) %all-to-all-start.1) | async-done | bytes 131104 | tf_op jit(solution)/shard_map/all_to_all | solution.py:263
  88.6 4.0 %collective-permute-start = (bf16[512,128]{1,0:T(8,128)(2,1)S(1)}, bf16[512,128]{1,0:T(8,128)(2,1)S(1)}, u32[]{:S(2)}, u32[]{:S(2)}) collective-permute-start(bf16[512,128]{1,0:T(8,128)(2,1)S(1)} %bitcast.18), channel_id=1, source_target_pairs={{0,4},{4,0},{1,5},{5,1},{2,6},{6,2},{3,7},{7,3},{8,12},{12,8},{9,1... | collective-permute-start | bytes 393224 | tf_op jit(solution)/shard_map/ppermute | solution.py:280
  92.6 1.0 %collective-permute-done.mate_ref = bf16[512,128]{1,0:T(8,128)(2,1)S(1)} collective-permute-done((bf16[512,128]{1,0:T(8,128)(2,1)S(1)}, bf16[512,128]{1,0:T(8,128)(2,1)S(1)}, u32[]{:S(2)}, u32[]{:S(2)}) %collective-permute-start) | collective-permute-done | bytes 131104 | tf_op jit(solution)/shard_map/ppermute | solution.py:280
  93.6 0.9 shard_map.132
  (1 shorter events, 0.0 us)
Async XLA Ops:
  0.6 0.7 copy-start.6
  1.4 1.0 %copy-start = (s32[768,16]{0,1:T(8,128)S(1)}, s32[768,16]{0,1:T(8,128)}, u32[]{:S(2)}) copy-start(s32[768,16]{0,1:T(8,128)} %param.13) | copy-start | bytes 147460
  1.4 1.0 %copy-start.1 = (bf16[768,256]{1,0:T(8,128)(2,1)S(1)}, bf16[768,256]{1,0:T(8,128)(2,1)}, u32[]{:S(2)}) copy-start(bf16[768,256]{1,0:T(8,128)(2,1)} %hid_ref.1) | copy-start | bytes 1179652
  1.4 1.1 %copy-start.2 = (bf16[768,128]{1,0:T(8,128)(2,1)S(1)}, bf16[768,128]{1,0:T(8,128)(2,1)}, u32[]{:S(2)}) copy-start(bf16[768,128]{1,0:T(8,128)(2,1)} %out_ref.1) | copy-start | bytes 589828
  1.4 1.2 %copy-start.3 = (bf16[768,128]{1,0:T(8,128)(2,1)S(1)}, bf16[768,128]{1,0:T(8,128)(2,1)}, u32[]{:S(2)}) copy-start(bf16[768,128]{1,0:T(8,128)(2,1)} %saved_ref.1) | copy-start | bytes 589828
  1.4 1.2 %copy-start.4 = (bf16[256,128]{1,0:T(8,128)(2,1)S(1)}, bf16[256,128]{1,0:T(8,128)(2,1)}, u32[]{:S(2)}) copy-start(bf16[256,128]{1,0:T(8,128)(2,1)} %w2_ref.1) | copy-start | bytes 196612
  1.4 1.2 %copy-start.5 = (bf16[128,256]{1,0:T(8,128)(2,1)S(1)}, bf16[128,256]{1,0:T(8,128)(2,1)}, u32[]{:S(2)}) copy-start(bf16[128,256]{1,0:T(8,128)(2,1)} %w1_ref.1) | copy-start | bytes 196612
  1.4 1.1 %copy-start.7 = (s32[1,1,128,4,8]{2,4,3,1,0:T(8,128)S(1)}, s32[1,1,128,4,8]{2,4,3,1,0:T(8,128)}, u32[]{:S(2)}) copy-start(s32[1,1,128,4,8]{2,4,3,1,0:T(8,128)} %param.14) | copy-start | bytes 49156
  64.9 12.0 %copy-start.8 = (s32[1,1,128,4,8]{2,4,3,1,0:T(8,128)S(1)}, s32[1,1,128,4,8]{2,4,3,1,0:T(8,128)}, u32[]{:S(2)}) copy-start(s32[1,1,128,4,8]{2,4,3,1,0:T(8,128)} %param.15) | copy-start | bytes 49156
  65.9 22.7 %all-to-all-start.1 = ((bf16[256,1,2,128]{3,2,1,0:T(2,128)(2,1)}), bf16[256,1,2,128]{3,2,1,0:T(2,128)(2,1)S(1)}, u32[]{:S(2)}, u32[]{:S(2)}) async-start(bf16[256,1,2,128]{3,2,1,0:T(2,128)(2,1)} %bitcast.7), calls=%async_computation.1 | async-start | bytes 262144 | tf_op jit(solution)/shard_map/all_to_all | solution.py:263
  88.6 5.0 %collective-permute-start = (bf16[512,128]{1,0:T(8,128)(2,1)S(1)}, bf16[512,128]{1,0:T(8,128)(2,1)S(1)}, u32[]{:S(2)}, u32[]{:S(2)}) collective-permute-start(bf16[512,128]{1,0:T(8,128)(2,1)S(1)} %bitcast.18), channel_id=1, source_target_pairs={{0,4},{4,0},{1,5},{5,1},{2,6},{6,2},{3,7},{7,3},{8,12},{12,8},{9,1... | collective-permute-start | bytes 393224 | tf_op jit(solution)/shard_map/ppermute | solution.py:280

commit v7 on v5

--- a/solution.py
+++ b/solution.py
@@ -84,6 +84,7 @@
     out = out_ref[...]
     hidden = hid_ref[...]
     grad_hidden = dot(out, w2_ref[...], LAST)
+    part_w2 = dot(out, hidden, FIRST)
     grad_z = jnp.where(hidden > 0, grad_hidden, 0.0).astype(BF16)
     grad_agg = dot(grad_z, w1_ref[...], LAST)
     wire = grad_agg.astype(BF16)
@@ -109,7 +110,6 @@
     node = jnp.sum(grad_agg, axis=0, keepdims=True) + jnp.sum(carried, axis=0, keepdims=True)
 
     part_w1 = dot(saved_ref[...], grad_z, FIRST)
-    part_w2 = dot(out, hidden, FIRST)
     sum_z = jnp.sum(grad_z.astype(F32), axis=0, keepdims=True)
     sum_out = jnp.sum(out.astype(F32), axis=0, keepdims=True)
     quarters = [
@@ -173,8 +173,9 @@
 
 
 def last_kernel(share_ref, w1_ref, b1_ref, w2_ref, b2_ref, node_ref, rows_ref):
-    rows_ref[...] = share_ref[...].astype(F32)
-    half = rows_ref.shape[0] // 2
+    count = share_ref.shape[0]
+    half = count // 2
+    rows_ref[:count, :] = share_ref[...].astype(F32)
     high = rows_ref[pl.ds(0, half, 2), :]
     low = rows_ref[pl.ds(1, half, 2), :]
     lane = iota(high.shape, 1)
@@ -271,7 +272,7 @@
             ((1, width), F32),
             ((1, width), F32),
         ],
-        [pltpu.VMEM((devices * EXTRA, width), F32)],
+        [pltpu.VMEM((devices * EXTRA + 8, width), F32)],
         flops=0,
         bytes_accessed=devices * EXTRA * width * 2,
     )(shares)

time: 93.2 us -> 93.1 us (level)
  no operation moved by 1% of the time
where the time goes in v7:
time: 93.1 us; the launch traced here: 92.8 us
  blocking collectives  59.7 us (64%)
  Pallas kernels  10.7 us (11%)
  waiting for transfers between devices  10.7 us (11%)
  starting transfers between devices  9.67 us (10%)
  local copies, waits for them, and re-layouts  1.33 us (1%)
    all_to_all x1, blocking collectives, exchange(): lax.all_to_all(x, AXES, split_axis=0, concat_axis=0, tiled=True)  59.7 us
    all_to_all x1, waiting for transfers between devices, exchange(): lax.all_to_all(x, AXES, split_axis=0, concat_axis=0, tiled=True)  10.7 us
    all_to_all x1, starting transfers between devices, exchange(): lax.all_to_all(x, AXES, split_axis=0, concat_axis=0, tiled=True)  9.67 us
    pallas_call x1, Pallas kernels, per_device(): call(remote_kernel, [((rows, width), BF16)], flops=2 * devices * piece *...  2.87 us
    pallas_call x1, Pallas kernels, per_device(): call(first_kernel, [((devices * piece, width), BF16), ((rows, width), F32...  2.52 us
    pallas_call x1, Pallas kernels, per_device(): call(local_kernel, [((rows, width), F32), ((devices * piece // LANES, LAN...  2.4 us
  transfers between devices with their start and end apart: 1, of which 1 were waited for; matrix products, arithmetic and copies ran while one was open for 1% of the time, Pallas kernels for 6%

profile of v7, /device:TPU:1, one launch (start us, length us, event | category | flops | bytes accessed | tf_op | source)
XLA Modules:
  0.0 92.8 jit_solution(9364078719023246770)
XLA Ops:
  0.6 0.0 copy-start.6
  0.6 0.7 copy-done.6
  1.4 0.0 copy-start
  1.4 0.0 copy-start.1
  1.4 0.0 copy-start.2
  1.4 0.0 copy-start.3
  1.4 0.0 copy-start.4
  1.4 0.0 copy-start.5
  1.4 0.0 copy-start.7
  1.4 1.0 %shard_map.127 = (bf16[2,1280,512]{2,1,0:T(8,128)(2,1)S(1)}, s16[2,1280,128]{2,1,0:T(8,128)(2,1)S(1)}) custom-call(s32[4,8,128]{2,1,0:T(8,128)S(1)} %bitcast.20), custom_call_target="tpu_custom_call" | custom-call | flops 2000000000 | bytes 2621440 | tf_op jit(solution)/shard_map/pallas_call | solution.py:223
  2.4 0.0 copy-done
  2.4 0.0 copy-done.1
  2.4 0.0 copy-done.2
  2.4 0.1 copy-done.3
  2.5 0.0 copy-done.4
  2.5 0.0 copy-done.5
  2.5 0.0 copy-done.7
  2.5 2.5 %shard_map.128 = (bf16[5120,128]{1,0:T(8,128)(2,1)S(1)}, f32[768,128]{1,0:T(8,128)S(1)}, bf16[768,128]{1,0:T(8,128)(2,1)S(1)}) custom-call(bf16[2,1280,512]{2,1,0:T(8,128)(2,1)S(1)} %get-tuple-element.18.chosen_ref, s16[2,1280,128]{2,1,0:T(8,128)(2,1)S(1)} %get-tuple-element.19.index_ref, s32[4,8,128]{2,1,0:T(8,128)S(1)} %bitcast.21, ...), custom_call_target="tpu_custom_call" | custom-call | flops 1342177280 | bytes 5242880 | tf_op jit(solution)/shard_map/pallas_call | solution.py:230
  5.1 59.7 %all_to_all.10 = bf16[512,5,2,128]{3,2,1,0:T(2,128)(2,1)S(1)} all-to-all(bf16[512,5,2,128]{3,2,1,0:T(2,128)(2,1)S(1)} %bitcast.16), channel_id=1, replica_groups=mesh['nodes'=128,'grp'=4] {'nodes','grp'}, dimensions={0} | all-to-all | bytes 2621440 | tf_op jit(solution)/shard_map/all_to_all | solution.py:250
  64.8 0.0 copy-start.8
  64.8 1.1 %shard_map.131 = bf16[1024,128]{1,0:T(8,128)(2,1)} custom-call(bf16[5120,128]{1,0:T(8,128)(2,1)S(1)} %bitcast.14), custom_call_target="tpu_custom_call" | custom-call | flops 20971520 | bytes 1310720 | tf_op jit(solution)/shard_map/pallas_call | solution.py:253
  65.9 9.7 %all-to-all-start.1 = ((bf16[512,1,2,128]{3,2,1,0:T(2,128)(2,1)}), bf16[512,1,2,128]{3,2,1,0:T(2,128)(2,1)S(1)}, u32[]{:S(2)}, u32[]{:S(2)}) async-start(bf16[512,1,2,128]{3,2,1,0:T(2,128)(2,1)} %bitcast.7), calls=%async_computation.1 | async-start | bytes 524288 | tf_op jit(solution)/shard_map/all_to_all | solution.py:250
  75.5 0.0 copy-done.8
  75.6 0.1 copy.18
  75.8 0.3 reshape.27.recv_ref
  76.0 2.4 %shard_map.129 = (f32[768,128]{1,0:T(8,128)S(1)}, s32[40,128]{1,0:T(8,128)S(1)}) custom-call(s32[16,768]{1,0:T(8,128)S(1)} %bitcast.19, s32[40,128]{1,0:T(8,128)S(1)} %reshape.27.recv_ref, bf16[768,128]{1,0:T(8,128)(2,1)S(1)} %get-tuple-element.20.wire_ref, f32[768,128]{1,0:T(8,128)S(1)} %get-tuple-element.21.agg_ref), custom_call_target="tpu_custom_call" | custom-call | flops 150994944 | bytes 983040 | tf_op jit(solution)/shard_map/pallas_call | solution.py:240
  78.4 2.9 %shard_map.130 = bf16[768,128]{1,0:T(8,128)(2,1)} custom-call(s32[40,128]{1,0:T(8,128)S(1)} %get-tuple-element.22.recv_ref, bf16[5120,128]{1,0:T(8,128)(2,1)S(1)} %bitcast.15, f32[768,128]{1,0:T(8,128)S(1)} %get-tuple-element.24.total_ref), custom_call_target="tpu_custom_call" | custom-call | flops 1006632960 | bytes 1310720 | tf_op jit(solution)/shard_map/pallas_call | solution.py:260
  81.3 10.7 %all-to-all-done.1 = bf16[512,1,2,128]{3,2,1,0:T(2,128)(2,1)S(1)} async-done(((bf16[512,1,2,128]{3,2,1,0:T(2,128)(2,1)}), bf16[512,1,2,128]{3,2,1,0:T(2,128)(2,1)S(1)}, u32[]{:S(2)}, u32[]{:S(2)}) %all-to-all-start.1) | async-done | bytes 262176 | tf_op jit(solution)/shard_map/all_to_all | solution.py:250
  92.0 0.8 shard_map.132
  (1 shorter events, 0.0 us)
Async XLA Ops:
  0.6 0.7 copy-start.6
  1.4 1.0 %copy-start = (s32[768,16]{0,1:T(8,128)S(1)}, s32[768,16]{0,1:T(8,128)}, u32[]{:S(2)}) copy-start(s32[768,16]{0,1:T(8,128)} %param.13) | copy-start | bytes 147460
  1.4 1.0 %copy-start.1 = (bf16[768,256]{1,0:T(8,128)(2,1)S(1)}, bf16[768,256]{1,0:T(8,128)(2,1)}, u32[]{:S(2)}) copy-start(bf16[768,256]{1,0:T(8,128)(2,1)} %hid_ref.1) | copy-start | bytes 1179652
  1.4 1.1 %copy-start.2 = (bf16[768,128]{1,0:T(8,128)(2,1)S(1)}, bf16[768,128]{1,0:T(8,128)(2,1)}, u32[]{:S(2)}) copy-start(bf16[768,128]{1,0:T(8,128)(2,1)} %out_ref.1) | copy-start | bytes 589828
  1.4 1.2 %copy-start.3 = (bf16[768,128]{1,0:T(8,128)(2,1)S(1)}, bf16[768,128]{1,0:T(8,128)(2,1)}, u32[]{:S(2)}) copy-start(bf16[768,128]{1,0:T(8,128)(2,1)} %saved_ref.1) | copy-start | bytes 589828
  1.4 1.2 %copy-start.4 = (bf16[256,128]{1,0:T(8,128)(2,1)S(1)}, bf16[256,128]{1,0:T(8,128)(2,1)}, u32[]{:S(2)}) copy-start(bf16[256,128]{1,0:T(8,128)(2,1)} %w2_ref.1) | copy-start | bytes 196612
  1.4 1.2 %copy-start.5 = (bf16[128,256]{1,0:T(8,128)(2,1)S(1)}, bf16[128,256]{1,0:T(8,128)(2,1)}, u32[]{:S(2)}) copy-start(bf16[128,256]{1,0:T(8,128)(2,1)} %w1_ref.1) | copy-start | bytes 196612
  1.4 1.1 %copy-start.7 = (s32[1,1,128,4,8]{2,4,3,1,0:T(8,128)S(1)}, s32[1,1,128,4,8]{2,4,3,1,0:T(8,128)}, u32[]{:S(2)}) copy-start(s32[1,1,128,4,8]{2,4,3,1,0:T(8,128)} %param.14) | copy-start | bytes 49156
  64.8 10.8 %copy-start.8 = (s32[1,1,128,4,8]{2,4,3,1,0:T(8,128)S(1)}, s32[1,1,128,4,8]{2,4,3,1,0:T(8,128)}, u32[]{:S(2)}) copy-start(s32[1,1,128,4,8]{2,4,3,1,0:T(8,128)} %param.15) | copy-start | bytes 49156
  65.9 26.1 %all-to-all-start.1 = ((bf16[512,1,2,128]{3,2,1,0:T(2,128)(2,1)}), bf16[512,1,2,128]{3,2,1,0:T(2,128)(2,1)S(1)}, u32[]{:S(2)}, u32[]{:S(2)}) async-start(bf16[512,1,2,128]{3,2,1,0:T(2,128)(2,1)} %bitcast.7), calls=%async_computation.1 | async-start | bytes 524288 | tf_op jit(solution)/shard_map/all_to_all | solution.py:250

commit v8 on v7

--- a/solution.py
+++ b/solution.py
@@ -49,10 +49,8 @@
     block = chosen_ref.shape[1]
     piece = slots + EXTRA
     width = LANES // groups
-    place = jnp.where(
-        iota((block, LANES), 0) // piece * piece == piece * iota((block, LANES), 1), 1.0, 0.0
-    )
-    place = jnp.where(iota((block, LANES), 0) % piece >= slots, place, 0.0).astype(BF16)
+    row = iota((block, LANES), 0) - (piece * iota((1, LANES), 1) + slots)
+    place = jnp.where(row >> 1 == 0, 1.0, 0.0).astype(BF16)
     parts = []
     for g in range(groups):
         parts += [send_ref[g], jnp.full((1, nodes), -1, jnp.int32), jnp.full((1, nodes), 4 * half, jnp.int32)]
@@ -215,7 +213,7 @@
     send = jnp.transpose(send_slots[0, 0], (1, 2, 0))
     blocks = devices // LANES
     depth = rows // 2 + LANES
-    early = blocks // 2
+    early = blocks - blocks // 4
 
     def shapes(n):
         return [((n, LANES * piece, depth), BF16), ((n, LANES * piece, LANES), jnp.int16)]

time: 93.1 us -> 93 us (level)
  no operation moved by 1% of the time
where the time goes in v8:
time: 93 us; the launch traced here: 92.7 us
  blocking collectives  59.7 us (64%)
  waiting for transfers between devices  10.7 us (12%)
  Pallas kernels  10.6 us (11%)
  starting transfers between devices  9.67 us (10%)
  local copies, waits for them, and re-layouts  1.34 us (1%)
    all_to_all x1, blocking collectives, exchange(): lax.all_to_all(x, AXES, split_axis=0, concat_axis=0, tiled=True)  59.7 us
    all_to_all x1, waiting for transfers between devices, exchange(): lax.all_to_all(x, AXES, split_axis=0, concat_axis=0, tiled=True)  10.7 us
    all_to_all x1, starting transfers between devices, exchange(): lax.all_to_all(x, AXES, split_axis=0, concat_axis=0, tiled=True)  9.67 us
    pallas_call x1, Pallas kernels, per_device(): call(remote_kernel, [((rows, width), BF16)], flops=2 * devices * piece *...  2.87 us
    pallas_call x1, Pallas kernels, per_device(): call(local_kernel, [((rows, width), F32), ((devices * piece // LANES, LAN...  2.4 us
    pallas_call x1, Pallas kernels, per_device(): call(first_kernel, [((devices * piece, width), BF16), ((rows, width), F32...  2.39 us
  transfers between devices with their start and end apart: 1, of which 1 were waited for; matrix products, arithmetic and copies ran while one was open for 1% of the time, Pallas kernels for 6%

profile of v8, /device:TPU:1, one launch (start us, length us, event | category | flops | bytes accessed | tf_op | source)
XLA Modules:
  0.0 92.7 jit_solution(834758145155358881)
XLA Ops:
  0.6 0.0 copy-start.6
  0.6 0.7 copy-done.6
  1.4 0.0 copy-start
  1.4 0.0 copy-start.1
  1.4 0.0 copy-start.2
  1.4 0.0 copy-start.3
  1.4 0.0 copy-start.4
  1.4 0.0 copy-start.5
  1.4 0.0 copy-start.7
  1.4 1.0 %shard_map.127 = (bf16[3,1280,512]{2,1,0:T(8,128)(2,1)S(1)}, s16[3,1280,128]{2,1,0:T(8,128)(2,1)S(1)}) custom-call(s32[4,8,128]{2,1,0:T(8,128)S(1)} %bitcast.20), custom_call_target="tpu_custom_call" | custom-call | flops 2000000000 | bytes 3932160 | tf_op jit(solution)/shard_map/pallas_call | solution.py:221
  2.4 0.0 copy-done
  2.4 0.0 copy-done.1
  2.4 0.0 copy-done.2
  2.4 0.1 copy-done.3
  2.5 0.0 copy-done.4
  2.5 0.0 copy-done.5
  2.5 0.0 copy-done.7
  2.5 2.4 %shard_map.128 = (bf16[5120,128]{1,0:T(8,128)(2,1)S(1)}, f32[768,128]{1,0:T(8,128)S(1)}, bf16[768,128]{1,0:T(8,128)(2,1)S(1)}) custom-call(bf16[3,1280,512]{2,1,0:T(8,128)(2,1)S(1)} %get-tuple-element.18.chosen_ref, s16[3,1280,128]{2,1,0:T(8,128)(2,1)S(1)} %get-tuple-element.19.index_ref, s32[4,8,128]{2,1,0:T(8,128)S(1)} %bitcast.21, ...), custom_call_target="tpu_custom_call" | custom-call | flops 1342177280 | bytes 5242880 | tf_op jit(solution)/shard_map/pallas_call | solution.py:228
  4.9 59.7 %all_to_all.10 = bf16[512,5,2,128]{3,2,1,0:T(2,128)(2,1)S(1)} all-to-all(bf16[512,5,2,128]{3,2,1,0:T(2,128)(2,1)S(1)} %bitcast.16), channel_id=1, replica_groups=mesh['nodes'=128,'grp'=4] {'nodes','grp'}, dimensions={0} | all-to-all | bytes 2621440 | tf_op jit(solution)/shard_map/all_to_all | solution.py:248
  64.6 0.0 copy-start.8
  64.6 1.1 %shard_map.131 = bf16[1024,128]{1,0:T(8,128)(2,1)} custom-call(bf16[5120,128]{1,0:T(8,128)(2,1)S(1)} %bitcast.14), custom_call_target="tpu_custom_call" | custom-call | flops 20971520 | bytes 1310720 | tf_op jit(solution)/shard_map/pallas_call | solution.py:251
  65.7 9.7 %all-to-all-start.1 = ((bf16[512,1,2,128]{3,2,1,0:T(2,128)(2,1)}), bf16[512,1,2,128]{3,2,1,0:T(2,128)(2,1)S(1)}, u32[]{:S(2)}, u32[]{:S(2)}) async-start(bf16[512,1,2,128]{3,2,1,0:T(2,128)(2,1)} %bitcast.7), calls=%async_computation.1 | async-start | bytes 524288 | tf_op jit(solution)/shard_map/all_to_all | solution.py:248
  75.4 0.0 copy-done.8
  75.4 0.1 copy.18
  75.6 0.3 reshape.27.recv_ref
  75.9 2.4 %shard_map.129 = (f32[768,128]{1,0:T(8,128)S(1)}, s32[40,128]{1,0:T(8,128)S(1)}) custom-call(s32[16,768]{1,0:T(8,128)S(1)} %bitcast.19, s32[40,128]{1,0:T(8,128)S(1)} %reshape.27.recv_ref, bf16[768,128]{1,0:T(8,128)(2,1)S(1)} %get-tuple-element.20.wire_ref, f32[768,128]{1,0:T(8,128)S(1)} %get-tuple-element.21.agg_ref), custom_call_target="tpu_custom_call" | custom-call | flops 150994944 | bytes 983040 | tf_op jit(solution)/shard_map/pallas_call | solution.py:238
  78.3 2.9 %shard_map.130 = bf16[768,128]{1,0:T(8,128)(2,1)} custom-call(s32[40,128]{1,0:T(8,128)S(1)} %get-tuple-element.22.recv_ref, bf16[5120,128]{1,0:T(8,128)(2,1)S(1)} %bitcast.15, f32[768,128]{1,0:T(8,128)S(1)} %get-tuple-element.24.total_ref), custom_call_target="tpu_custom_call" | custom-call | flops 1006632960 | bytes 1310720 | tf_op jit(solution)/shard_map/pallas_call | solution.py:258
  81.2 10.7 %all-to-all-done.1 = bf16[512,1,2,128]{3,2,1,0:T(2,128)(2,1)S(1)} async-done(((bf16[512,1,2,128]{3,2,1,0:T(2,128)(2,1)}), bf16[512,1,2,128]{3,2,1,0:T(2,128)(2,1)S(1)}, u32[]{:S(2)}, u32[]{:S(2)}) %all-to-all-start.1) | async-done | bytes 262176 | tf_op jit(solution)/shard_map/all_to_all | solution.py:248
  91.9 0.8 shard_map.132
  (1 shorter events, 0.0 us)
Async XLA Ops:
  0.6 0.7 copy-start.6
  1.4 1.0 %copy-start = (bf16[768,256]{1,0:T(8,128)(2,1)S(1)}, bf16[768,256]{1,0:T(8,128)(2,1)}, u32[]{:S(2)}) copy-start(bf16[768,256]{1,0:T(8,128)(2,1)} %hid_ref.1) | copy-start | bytes 1179652
  1.4 1.0 %copy-start.1 = (s32[768,16]{0,1:T(8,128)S(1)}, s32[768,16]{0,1:T(8,128)}, u32[]{:S(2)}) copy-start(s32[768,16]{0,1:T(8,128)} %param.13) | copy-start | bytes 147460
  1.4 1.1 %copy-start.2 = (bf16[768,128]{1,0:T(8,128)(2,1)S(1)}, bf16[768,128]{1,0:T(8,128)(2,1)}, u32[]{:S(2)}) copy-start(bf16[768,128]{1,0:T(8,128)(2,1)} %out_ref.1) | copy-start | bytes 589828
  1.4 1.2 %copy-start.3 = (bf16[768,128]{1,0:T(8,128)(2,1)S(1)}, bf16[768,128]{1,0:T(8,128)(2,1)}, u32[]{:S(2)}) copy-start(bf16[768,128]{1,0:T(8,128)(2,1)} %saved_ref.1) | copy-start | bytes 589828
  1.4 1.2 %copy-start.4 = (bf16[256,128]{1,0:T(8,128)(2,1)S(1)}, bf16[256,128]{1,0:T(8,128)(2,1)}, u32[]{:S(2)}) copy-start(bf16[256,128]{1,0:T(8,128)(2,1)} %w2_ref.1) | copy-start | bytes 196612
  1.4 1.1 %copy-start.5 = (bf16[128,256]{1,0:T(8,128)(2,1)S(1)}, bf16[128,256]{1,0:T(8,128)(2,1)}, u32[]{:S(2)}) copy-start(bf16[128,256]{1,0:T(8,128)(2,1)} %w1_ref.1) | copy-start | bytes 196612
  1.4 1.1 %copy-start.7 = (s32[1,1,128,4,8]{2,4,3,1,0:T(8,128)S(1)}, s32[1,1,128,4,8]{2,4,3,1,0:T(8,128)}, u32[]{:S(2)}) copy-start(s32[1,1,128,4,8]{2,4,3,1,0:T(8,128)} %param.14) | copy-start | bytes 49156
  64.6 10.8 %copy-start.8 = (s32[1,1,128,4,8]{2,4,3,1,0:T(8,128)S(1)}, s32[1,1,128,4,8]{2,4,3,1,0:T(8,128)}, u32[]{:S(2)}) copy-start(s32[1,1,128,4,8]{2,4,3,1,0:T(8,128)} %param.15) | copy-start | bytes 49156
  65.7 26.1 %all-to-all-start.1 = ((bf16[512,1,2,128]{3,2,1,0:T(2,128)(2,1)}), bf16[512,1,2,128]{3,2,1,0:T(2,128)(2,1)S(1)}, u32[]{:S(2)}, u32[]{:S(2)}) async-start(bf16[512,1,2,128]{3,2,1,0:T(2,128)(2,1)} %bitcast.7), calls=%async_computation.1 | async-start | bytes 524288 | tf_op jit(solution)/shard_map/all_to_all | solution.py:248

commit v9 on v8

--- a/solution.py
+++ b/solution.py
@@ -128,20 +128,6 @@
         )
 
 
-def local_kernel(lists_ref, recv_ref, wire_ref, agg_ref, total_ref, target_ref, counts_ref):
-    rows = wire_ref.shape[0]
-    row_index = iota((rows, 1), 0).astype(jnp.int16)
-    for tile in range(rows // LANES):
-        lists = lists_ref[:, tile * LANES : (tile + 1) * LANES].astype(jnp.int16)
-        counts = match(lists[0:1], row_index)
-        for k in range(1, lists_ref.shape[0]):
-            counts += match(lists[k : k + 1], row_index)
-        counts_ref[:, tile * LANES : (tile + 1) * LANES] = counts
-    local = dot(wire_ref[...].T, counts_ref[...])
-    total_ref[...] = agg_ref[...] + local.T
-    target_ref[...] = recv_ref[...]
-
-
 def chunk_kernel(piece, scale, arrived_ref, share_ref):
     span = piece * LANES
     lane = iota((16, span), 1)
@@ -159,11 +145,17 @@
     share_ref[...] = jnp.concatenate([pair] * (share_ref.shape[0] // EXTRA), axis=0)
 
 
-def remote_kernel(recv_ref, arrived_ref, total_ref, x_ref):
-    rows = total_ref.shape[0]
+def edges_kernel(lists_ref, recv_ref, wire_ref, agg_ref, arrived_ref, x_ref, counts_ref):
+    rows = wire_ref.shape[0]
     row_index = iota((rows, 1), 0).astype(jnp.int16)
+    for tile in range(rows // LANES):
+        lists = lists_ref[:, tile * LANES : (tile + 1) * LANES].astype(jnp.int16)
+        counts = match(lists[0:1], row_index)
+        for k in range(1, lists_ref.shape[0]):
+            counts += match(lists[k : k + 1], row_index)
+        counts_ref[:, tile * LANES : (tile + 1) * LANES] = counts
+    total = agg_ref[...] + dot(wire_ref[...].T, counts_ref[...]).T
     targets = recv_ref[...].astype(jnp.int16)
-    total = total_ref[...]
     for r in range(0, recv_ref.shape[0], 2):
         chosen = jnp.concatenate([match(targets[q : q + 1], row_index) for q in (r, r + 1)], axis=1)
         total += dot(chosen, arrived_ref[r * LANES : (r + 2) * LANES, :])
@@ -235,14 +227,6 @@
         bytes_accessed=devices * piece * depth * 2,
     )(chosen, index, send, grad_out, w_two, hidden_saved, w_one, lists, agg_saved)
     recv = jnp.pad(receive_slots[0, 0], ((0, 0), (0, 0), (0, EXTRA)), constant_values=rows)
-    total, targets = call(
-        local_kernel,
-        [((rows, width), F32), ((devices * piece // LANES, LANES), jnp.int32)],
-        [pltpu.VMEM((rows, rows), BF16)],
-        flops=2 * rows * rows * width,
-        bytes_accessed=rows * width * 10,
-    )(lists, recv.reshape(-1, LANES), wire, agg)
-
     def exchange(x, height):
         x = x.reshape(devices, height // 2, 2, width)
         return lax.all_to_all(x, AXES, split_axis=0, concat_axis=0, tiled=True).reshape(-1, width)
@@ -256,11 +240,12 @@
     )(arrived)
     shares = exchange(share, EXTRA)
     (grad_x,) = call(
-        remote_kernel,
+        edges_kernel,
         [((rows, width), BF16)],
-        flops=2 * devices * piece * rows * width,
+        [pltpu.VMEM((rows, rows), BF16)],
+        flops=2 * (devices * piece + rows) * rows * width,
         bytes_accessed=devices * piece * width * 2,
-    )(targets, arrived, total)
+    )(lists, recv.reshape(-1, LANES), wire, agg, arrived)
     w1, b1, w2, b2, node = call(
         last_kernel,
         [

time: 93 us -> 92.9 us (level)
    pallas_call x2 -> x1, Pallas kernels: 5.26 us -> 4.99 us  [per_device(): call(edges_kernel, [((rows, width), BF16)], [pltpu.VMEM((rows, rows), BF1...]
  transfers between devices with their start and end apart: 1 -> 1, of which waited for: 1 -> 1; matrix products, arithmetic and copies ran while one was open for 1% -> 1% of each run, Pallas kernels for 6% -> 5%
where the time goes in v9:
time: 92.9 us; the launch traced here: 92.7 us
  blocking collectives  59.7 us (64%)
  waiting for transfers between devices  10.9 us (12%)
  Pallas kernels  10.3 us (11%)
  starting transfers between devices  9.67 us (10%)
  local copies, waits for them, and re-layouts  1.34 us (1%)
    all_to_all x1, blocking collectives, exchange(): lax.all_to_all(x, AXES, split_axis=0, concat_axis=0, tiled=True)  59.7 us
    all_to_all x1, waiting for transfers between devices, exchange(): lax.all_to_all(x, AXES, split_axis=0, concat_axis=0, tiled=True)  10.9 us
    all_to_all x1, starting transfers between devices, exchange(): lax.all_to_all(x, AXES, split_axis=0, concat_axis=0, tiled=True)  9.67 us
    pallas_call x1, Pallas kernels, per_device(): call(edges_kernel, [((rows, width), BF16)], [pltpu.VMEM((rows, rows), BF1...  4.99 us
    pallas_call x1, Pallas kernels, per_device(): call(first_kernel, [((devices * piece, width), BF16), ((rows, width), F32...  2.4 us
  transfers between devices with their start and end apart: 1, of which 1 were waited for; matrix products, arithmetic and copies ran while one was open for 1% of the time, Pallas kernels for 5%

profile of v9, /device:TPU:1, one launch (start us, length us, event | category | flops | bytes accessed | tf_op | source)
XLA Modules:
  0.0 92.7 jit_solution(14974321430463557599)
XLA Ops:
  0.6 0.0 copy-start.6
  0.6 0.7 copy-done.6
  1.4 0.0 copy-start
  1.4 0.0 copy-start.1
  1.4 0.0 copy-start.2
  1.4 0.0 copy-start.3
  1.4 0.0 copy-start.4
  1.4 0.0 copy-start.5
  1.4 1.0 %shard_map.127 = (bf16[3,1280,512]{2,1,0:T(8,128)(2,1)S(1)}, s16[3,1280,128]{2,1,0:T(8,128)(2,1)S(1)}) custom-call(s32[4,8,128]{2,1,0:T(8,128)S(1)} %bitcast.20), custom_call_target="tpu_custom_call" | custom-call | flops 2000000000 | bytes 3932160 | tf_op jit(solution)/shard_map/pallas_call | solution.py:213
  2.3 0.0 copy-done
  2.4 0.0 copy-done.1
  2.4 0.1 copy-done.2
  2.5 0.0 copy-done.3
  2.5 0.0 copy-done.4
  2.5 0.0 copy-done.5
  2.5 2.4 %shard_map.128 = (bf16[5120,128]{1,0:T(8,128)(2,1)S(1)}, f32[768,128]{1,0:T(8,128)S(1)}, bf16[768,128]{1,0:T(8,128)(2,1)S(1)}) custom-call(bf16[3,1280,512]{2,1,0:T(8,128)(2,1)S(1)} %get-tuple-element.16.chosen_ref, s16[3,1280,128]{2,1,0:T(8,128)(2,1)S(1)} %get-tuple-element.17.index_ref, s32[4,8,128]{2,1,0:T(8,128)S(1)} %bitcast.21, ...), custom_call_target="tpu_custom_call" | custom-call | flops 1342177280 | bytes 5242880 | tf_op jit(solution)/shard_map/pallas_call | solution.py:220
  4.9 59.7 %all_to_all.10 = bf16[512,5,2,128]{3,2,1,0:T(2,128)(2,1)S(1)} all-to-all(bf16[512,5,2,128]{3,2,1,0:T(2,128)(2,1)S(1)} %bitcast.16), channel_id=1, replica_groups=mesh['nodes'=128,'grp'=4] {'nodes','grp'}, dimensions={0} | all-to-all | bytes 2621440 | tf_op jit(solution)/shard_map/all_to_all | solution.py:232
  64.6 0.0 copy-start.7
  64.6 1.1 %shard_map.130 = bf16[1024,128]{1,0:T(8,128)(2,1)} custom-call(bf16[5120,128]{1,0:T(8,128)(2,1)S(1)} %bitcast.14), custom_call_target="tpu_custom_call" | custom-call | flops 20971520 | bytes 1310720 | tf_op jit(solution)/shard_map/pallas_call | solution.py:235
  65.7 9.7 %all-to-all-start.1 = ((bf16[512,1,2,128]{3,2,1,0:T(2,128)(2,1)}), bf16[512,1,2,128]{3,2,1,0:T(2,128)(2,1)S(1)}, u32[]{:S(2)}, u32[]{:S(2)}) async-start(bf16[512,1,2,128]{3,2,1,0:T(2,128)(2,1)} %bitcast.7), calls=%async_computation.1 | async-start | bytes 524288 | tf_op jit(solution)/shard_map/all_to_all | solution.py:232
  75.4 0.0 copy-done.7
  75.4 0.1 copy.18
  75.6 0.3 reshape.27.recv_ref
  75.9 5.0 %shard_map.129 = bf16[768,128]{1,0:T(8,128)(2,1)} custom-call(s32[16,768]{1,0:T(8,128)S(1)} %bitcast.19, s32[40,128]{1,0:T(8,128)S(1)} %reshape.27.recv_ref, bf16[768,128]{1,0:T(8,128)(2,1)S(1)} %get-tuple-element.18.wire_ref, f32[768,128]{1,0:T(8,128)S(1)} %get-tuple-element.19.agg_ref, bf16[5120,128]{1,0:T(8,128)(2,1)S(1)} %bitcast.15), custom_call_target="tpu_custom_call" | custom-call | flops 1157627904 | bytes 1310720 | tf_op jit(solution)/shard_map/pallas_call | solution.py:242
  80.9 10.9 %all-to-all-done.1 = bf16[512,1,2,128]{3,2,1,0:T(2,128)(2,1)S(1)} async-done(((bf16[512,1,2,128]{3,2,1,0:T(2,128)(2,1)}), bf16[512,1,2,128]{3,2,1,0:T(2,128)(2,1)S(1)}, u32[]{:S(2)}, u32[]{:S(2)}) %all-to-all-start.1) | async-done | bytes 262176 | tf_op jit(solution)/shard_map/all_to_all | solution.py:232
  91.8 0.8 shard_map.131
  (1 shorter events, 0.0 us)
Async XLA Ops:
  0.6 0.7 copy-start.6
  1.4 1.0 %copy-start = (bf16[768,256]{1,0:T(8,128)(2,1)S(1)}, bf16[768,256]{1,0:T(8,128)(2,1)}, u32[]{:S(2)}) copy-start(bf16[768,256]{1,0:T(8,128)(2,1)} %hid_ref.1) | copy-start | bytes 1179652
  1.4 1.0 %copy-start.1 = (bf16[768,128]{1,0:T(8,128)(2,1)S(1)}, bf16[768,128]{1,0:T(8,128)(2,1)}, u32[]{:S(2)}) copy-start(bf16[768,128]{1,0:T(8,128)(2,1)} %out_ref.1) | copy-start | bytes 589828
  1.4 1.1 %copy-start.2 = (bf16[768,128]{1,0:T(8,128)(2,1)S(1)}, bf16[768,128]{1,0:T(8,128)(2,1)}, u32[]{:S(2)}) copy-start(bf16[768,128]{1,0:T(8,128)(2,1)} %saved_ref.1) | copy-start | bytes 589828
  1.4 1.1 %copy-start.3 = (bf16[256,128]{1,0:T(8,128)(2,1)S(1)}, bf16[256,128]{1,0:T(8,128)(2,1)}, u32[]{:S(2)}) copy-start(bf16[256,128]{1,0:T(8,128)(2,1)} %w2_ref.1) | copy-start | bytes 196612
  1.4 1.1 %copy-start.4 = (bf16[128,256]{1,0:T(8,128)(2,1)S(1)}, bf16[128,256]{1,0:T(8,128)(2,1)}, u32[]{:S(2)}) copy-start(bf16[128,256]{1,0:T(8,128)(2,1)} %w1_ref.1) | copy-start | bytes 196612
  1.4 1.1 %copy-start.5 = (s32[768,16]{0,1:T(8,128)S(1)}, s32[768,16]{0,1:T(8,128)}, u32[]{:S(2)}) copy-start(s32[768,16]{0,1:T(8,128)} %param.13) | copy-start | bytes 147460
  64.6 10.8 %copy-start.7 = (s32[1,1,128,4,8]{2,4,3,1,0:T(8,128)S(1)}, s32[1,1,128,4,8]{2,4,3,1,0:T(8,128)}, u32[]{:S(2)}) copy-start(s32[1,1,128,4,8]{2,4,3,1,0:T(8,128)} %param.15) | copy-start | bytes 49156
  65.7 26.1 %all-to-all-start.1 = ((bf16[512,1,2,128]{3,2,1,0:T(2,128)(2,1)}), bf16[512,1,2,128]{3,2,1,0:T(2,128)(2,1)S(1)}, u32[]{:S(2)}, u32[]{:S(2)}) async-start(bf16[512,1,2,128]{3,2,1,0:T(2,128)(2,1)} %bitcast.7), calls=%async_computation.1 | async-start | bytes 524288 | tf_op jit(solution)/shard_map/all_to_all | solution.py:232

commit v10 on v9

--- a/solution.py
+++ b/solution.py
@@ -96,8 +96,7 @@
     few = 32
     row_index = iota((few, 1), 0).astype(jnp.int16)
     count = jnp.zeros((few, few), F32)
-    for ref in [lists_ref] + [send_ref.at[g] for g in range(groups)]:
-        index = ref[...]
+    for index in (lists_ref[...], jnp.concatenate([send_ref[g] for g in range(groups)], axis=1)):
         low = (index & (few - 1)).astype(jnp.int16)
         high = (index >> 5).astype(jnp.int16)
         for k in range(index.shape[0]):

time: 92.9 us -> 92.8 us (level)
  no operation moved by 1% of the time
where the time goes in v10:
time: 92.8 us; the launch traced here: 92.5 us
  blocking collectives  59.7 us (64%)
  waiting for transfers between devices  10.9 us (12%)
  Pallas kernels  10.2 us (11%)
  starting transfers between devices  9.67 us (10%)
  local copies, waits for them, and re-layouts  1.34 us (1%)
    all_to_all x1, blocking collectives, exchange(): lax.all_to_all(x, AXES, split_axis=0, concat_axis=0, tiled=True)  59.7 us
    all_to_all x1, waiting for transfers between devices, exchange(): lax.all_to_all(x, AXES, split_axis=0, concat_axis=0, tiled=True)  10.9 us
    all_to_all x1, starting transfers between devices, exchange(): lax.all_to_all(x, AXES, split_axis=0, concat_axis=0, tiled=True)  9.67 us
    pallas_call x1, Pallas kernels, per_device(): call(edges_kernel, [((rows, width), BF16)], [pltpu.VMEM((rows, rows), BF1...  4.99 us
    pallas_call x1, Pallas kernels, per_device(): call(first_kernel, [((devices * piece, width), BF16), ((rows, width), F32...  2.3 us
  transfers between devices with their start and end apart: 1, of which 1 were waited for; matrix products, arithmetic and copies ran while one was open for 1% of the time, Pallas kernels for 5%

profile of v10, /device:TPU:1, one launch (start us, length us, event | category | flops | bytes accessed | tf_op | source)
XLA Modules:
  0.0 92.5 jit_solution(1054049049278220502)
XLA Ops:
  0.6 0.0 copy-start.6
  0.6 0.7 copy-done.6
  1.4 0.0 copy-start
  1.4 0.0 copy-start.1
  1.4 0.0 copy-start.2
  1.4 0.0 copy-start.3
  1.4 0.0 copy-start.4
  1.4 0.0 copy-start.5
  1.4 1.0 %shard_map.127 = (bf16[3,1280,512]{2,1,0:T(8,128)(2,1)S(1)}, s16[3,1280,128]{2,1,0:T(8,128)(2,1)S(1)}) custom-call(s32[4,8,128]{2,1,0:T(8,128)S(1)} %bitcast.20), custom_call_target="tpu_custom_call" | custom-call | flops 2000000000 | bytes 3932160 | tf_op jit(solution)/shard_map/pallas_call | solution.py:212
  2.3 0.0 copy-done
  2.4 0.0 copy-done.1
  2.4 0.1 copy-done.2
  2.5 0.0 copy-done.3
  2.5 0.0 copy-done.4
  2.5 0.0 copy-done.5
  2.5 2.3 %shard_map.128 = (bf16[5120,128]{1,0:T(8,128)(2,1)S(1)}, f32[768,128]{1,0:T(8,128)S(1)}, bf16[768,128]{1,0:T(8,128)(2,1)S(1)}) custom-call(bf16[3,1280,512]{2,1,0:T(8,128)(2,1)S(1)} %get-tuple-element.16.chosen_ref, s16[3,1280,128]{2,1,0:T(8,128)(2,1)S(1)} %get-tuple-element.17.index_ref, s32[4,8,128]{2,1,0:T(8,128)S(1)} %bitcast.21, ...), custom_call_target="tpu_custom_call" | custom-call | flops 1342177280 | bytes 5242880 | tf_op jit(solution)/shard_map/pallas_call | solution.py:219
  4.8 59.7 %all_to_all.10 = bf16[512,5,2,128]{3,2,1,0:T(2,128)(2,1)S(1)} all-to-all(bf16[512,5,2,128]{3,2,1,0:T(2,128)(2,1)S(1)} %bitcast.16), channel_id=1, replica_groups=mesh['nodes'=128,'grp'=4] {'nodes','grp'}, dimensions={0} | all-to-all | bytes 2621440 | tf_op jit(solution)/shard_map/all_to_all | solution.py:231
  64.5 0.0 copy-start.7
  64.5 1.1 %shard_map.130 = bf16[1024,128]{1,0:T(8,128)(2,1)} custom-call(bf16[5120,128]{1,0:T(8,128)(2,1)S(1)} %bitcast.14), custom_call_target="tpu_custom_call" | custom-call | flops 20971520 | bytes 1310720 | tf_op jit(solution)/shard_map/pallas_call | solution.py:234
  65.6 9.7 %all-to-all-start.1 = ((bf16[512,1,2,128]{3,2,1,0:T(2,128)(2,1)}), bf16[512,1,2,128]{3,2,1,0:T(2,128)(2,1)S(1)}, u32[]{:S(2)}, u32[]{:S(2)}) async-start(bf16[512,1,2,128]{3,2,1,0:T(2,128)(2,1)} %bitcast.7), calls=%async_computation.1 | async-start | bytes 524288 | tf_op jit(solution)/shard_map/all_to_all | solution.py:231
  75.3 0.0 copy-done.7
  75.3 0.1 copy.18
  75.5 0.3 reshape.27.recv_ref
  75.8 5.0 %shard_map.129 = bf16[768,128]{1,0:T(8,128)(2,1)} custom-call(s32[16,768]{1,0:T(8,128)S(1)} %bitcast.19, s32[40,128]{1,0:T(8,128)S(1)} %reshape.27.recv_ref, bf16[768,128]{1,0:T(8,128)(2,1)S(1)} %get-tuple-element.18.wire_ref, f32[768,128]{1,0:T(8,128)S(1)} %get-tuple-element.19.agg_ref, bf16[5120,128]{1,0:T(8,128)(2,1)S(1)} %bitcast.15), custom_call_target="tpu_custom_call" | custom-call | flops 1157627904 | bytes 1310720 | tf_op jit(solution)/shard_map/pallas_call | solution.py:241
  80.8 10.9 %all-to-all-done.1 = bf16[512,1,2,128]{3,2,1,0:T(2,128)(2,1)S(1)} async-done(((bf16[512,1,2,128]{3,2,1,0:T(2,128)(2,1)}), bf16[512,1,2,128]{3,2,1,0:T(2,128)(2,1)S(1)}, u32[]{:S(2)}, u32[]{:S(2)}) %all-to-all-start.1) | async-done | bytes 262176 | tf_op jit(solution)/shard_map/all_to_all | solution.py:231
  91.7 0.8 shard_map.131
  (1 shorter events, 0.0 us)
Async XLA Ops:
  0.6 0.7 copy-start.6
  1.4 1.0 %copy-start = (bf16[768,256]{1,0:T(8,128)(2,1)S(1)}, bf16[768,256]{1,0:T(8,128)(2,1)}, u32[]{:S(2)}) copy-start(bf16[768,256]{1,0:T(8,128)(2,1)} %hid_ref.1) | copy-start | bytes 1179652
  1.4 1.0 %copy-start.1 = (bf16[768,128]{1,0:T(8,128)(2,1)S(1)}, bf16[768,128]{1,0:T(8,128)(2,1)}, u32[]{:S(2)}) copy-start(bf16[768,128]{1,0:T(8,128)(2,1)} %out_ref.1) | copy-start | bytes 589828
  1.4 1.1 %copy-start.2 = (bf16[768,128]{1,0:T(8,128)(2,1)S(1)}, bf16[768,128]{1,0:T(8,128)(2,1)}, u32[]{:S(2)}) copy-start(bf16[768,128]{1,0:T(8,128)(2,1)} %saved_ref.1) | copy-start | bytes 589828
  1.4 1.1 %copy-start.3 = (bf16[256,128]{1,0:T(8,128)(2,1)S(1)}, bf16[256,128]{1,0:T(8,128)(2,1)}, u32[]{:S(2)}) copy-start(bf16[256,128]{1,0:T(8,128)(2,1)} %w2_ref.1) | copy-start | bytes 196612
  1.4 1.1 %copy-start.4 = (bf16[128,256]{1,0:T(8,128)(2,1)S(1)}, bf16[128,256]{1,0:T(8,128)(2,1)}, u32[]{:S(2)}) copy-start(bf16[128,256]{1,0:T(8,128)(2,1)} %w1_ref.1) | copy-start | bytes 196612
  1.4 1.1 %copy-start.5 = (s32[768,16]{0,1:T(8,128)S(1)}, s32[768,16]{0,1:T(8,128)}, u32[]{:S(2)}) copy-start(s32[768,16]{0,1:T(8,128)} %param.13) | copy-start | bytes 147460
  64.5 10.8 %copy-start.7 = (s32[1,1,128,4,8]{2,4,3,1,0:T(8,128)S(1)}, s32[1,1,128,4,8]{2,4,3,1,0:T(8,128)}, u32[]{:S(2)}) copy-start(s32[1,1,128,4,8]{2,4,3,1,0:T(8,128)} %param.15) | copy-start | bytes 49156
  65.6 26.1 %all-to-all-start.1 = ((bf16[512,1,2,128]{3,2,1,0:T(2,128)(2,1)}), bf16[512,1,2,128]{3,2,1,0:T(2,128)(2,1)S(1)}, u32[]{:S(2)}, u32[]{:S(2)}) async-start(bf16[512,1,2,128]{3,2,1,0:T(2,128)(2,1)} %bitcast.7), calls=%async_computation.1 | async-start | bytes 524288 | tf_op jit(solution)/shard_map/all_to_all | solution.py:231
